TPU v7x, 256 devices: a whole 4x4x8 slice. The times are simulated.
256 devices in a mesh: doc: 32 (over z, x), head: 8 (over y, core).
Axes of the slice: x: 4, y: 4, z: 8, core: 2. Of those that a mesh axis runs over, the one named last changes fastest.
Arguments:
- q_nope: bfloat16 [4096, 8192], P('doc', 'head'), may hold values from -6 to 6
- q_rope: bfloat16 [4096, 4096], P('doc', 'head'), may hold values from -8 to 8
- question_latent: bfloat16 [4096, 576], P('doc'), may hold values from -8 to 8
- doc_cache: bfloat16 [512, 512, 576], P('doc', 'head'), may hold values from -8 to 8
- w_uk: bfloat16 [64, 128, 512], P('head'), may hold values from -0.25 to 0.25
- w_uv: bfloat16 [64, 512, 128], P('head'), may hold values from -2 to 2
- doc_slot: int32 [512], replicated, may hold values from 0 to 511, as said below
- doc_blocks: int32 [512], replicated, may hold values from 1 to 4, 1280 in all
- pair_doc: int32 [1024], P('doc'), may hold values from 0 to 511, as said below
- pair_req: int32 [1024], P('doc'), may hold values from 0 to 7
Outputs:
- attn_values: bfloat16 [4096, 8192], P('doc', 'head')
Inputs may be any that keep to these rules, and one draw needn't show every extreme that they name: doc_slot is a permutation: every row of doc_cache holds exactly one document. `pair_doc`: pair k belongs to the index k // 32 of doc; no request names a document twice; the 32 pairs of one index of doc name at most 2 documents stored on any one index of doc, and in every draw some index of doc receives exactly 2 pairs from every index.
All inputs are finite; a program needn't handle non-finite values.
Results may differ from a plain program's by a relative error of at most 0.0065.
Values may be sent and summed in bfloat16 or wider, within the bound.
A program may use at most 256 MiB of HBM per device.

v0:
```python
import jax
import jax.numpy as jnp
from jax import lax
from jax.sharding import PartitionSpec as P

RANK = 512
ROPE = 64
NOPE = 128
VDIM = 128
Q_LEN = 16
BLOCK = 128


LOWEST = -1e30
slot_group = 8


def attend(queries, key_rows, visible, w_uv):
    score_scale = (NOPE + ROPE) ** (-0.5)
    scores = (
        jnp.einsum("bqhc,blc->bqhl", queries, key_rows, preferred_element_type=jnp.float32)
        * score_scale
    )
    key_mask = visible[:, :, None, :]
    scores = jnp.where(key_mask, scores, LOWEST)
    maxima = jnp.max(scores, axis=3)
    weights = jnp.where(key_mask, jnp.exp(scores - maxima[..., None]), 0.0)
    totals = jnp.sum(weights, axis=3)
    probabilities = weights.astype(jnp.bfloat16)
    latent = jnp.einsum(
        "bqhl,blc->bqhc", probabilities, key_rows[:, :, :RANK], preferred_element_type=jnp.float32
    ).astype(jnp.bfloat16)
    projected = jnp.einsum("bqhc,hcd->bqhd", latent, w_uv, preferred_element_type=jnp.float32)
    normed = (projected / totals[..., None]).astype(jnp.bfloat16)
    return (maxima, totals, normed)


def slot_partials(queries, table, picked, lengths, w_uv):
    slot_total = queries.shape[0]
    blocks = slot_total // slot_group
    places = jnp.arange(table.shape[1], dtype=jnp.int32)

    def one_block(inputs):
        block_queries, block_picked, block_lengths = inputs
        key_rows = jnp.take(table, block_picked, axis=0)
        visible = (places[None, :] < block_lengths[:, None])[:, None, :]
        return attend(block_queries, key_rows, visible, w_uv)

    grouped = (
        queries.reshape((blocks, slot_group) + queries.shape[1:]),
        picked.reshape(blocks, slot_group),
        lengths.reshape(blocks, slot_group),
    )
    maxima, totals, normed = lax.map(one_block, grouped)
    return (
        maxima.reshape((slot_total,) + maxima.shape[2:]),
        totals.reshape((slot_total,) + totals.shape[2:]),
        normed.reshape((slot_total,) + normed.shape[2:]),
    )


def absorb(nope_part, rope_part, w_uk):
    absorbed = jnp.einsum(
        "...hn,hnc->...hc", nope_part, w_uk, preferred_element_type=jnp.float32
    ).astype(jnp.bfloat16)
    return jnp.concatenate([absorbed, rope_part], axis=-1)


def on_device(
    q_nope, q_rope, question_latent, doc_cache, w_uk, w_uv, doc_slot, doc_blocks, pair_doc, pair_req
):
    head_count = w_uk.shape[0]
    tokens = q_nope.shape[0]
    requests = tokens // Q_LEN
    doc_dev = doc_cache.shape[0]
    latent_width = doc_cache.shape[2]
    peer_count = lax.axis_size("doc")
    pair_count = pair_doc.shape[0]
    capacity = max(2, 2 * pair_count // peer_count)
    slot_count = peer_count * capacity
    full_cache = lax.all_gather(doc_cache, "head", axis=1, tiled=True)
    queries = absorb(
        q_nope.reshape(tokens, head_count, NOPE), q_rope.reshape(tokens, head_count, ROPE), w_uk
    )
    doc_ids = jnp.arange(doc_slot.shape[0], dtype=jnp.int32)
    matches = pair_doc[:, None] == doc_ids[None, :]
    pair_slot = jnp.sum(jnp.where(matches, doc_slot[None, :], 0), axis=1)
    target = pair_slot // doc_dev
    local_doc = pair_slot % doc_dev
    pair_sequence = jnp.arange(pair_count, dtype=jnp.int32)
    before = (target[:, None] == target[None, :]) & (
        pair_sequence[None, :] < pair_sequence[:, None]
    )
    position = target * capacity + jnp.sum(before.astype(jnp.int32), axis=1)
    placed = jnp.arange(slot_count, dtype=jnp.int32)[:, None] == position[None, :]
    filled = jnp.sum(placed.astype(jnp.int32), axis=1)
    slot_request = jnp.sum(jnp.where(placed, pair_req[None, :], 0), axis=1)
    slot_local = jnp.sum(jnp.where(placed, local_doc[None, :], 0), axis=1)
    owners = (jnp.arange(requests, dtype=jnp.int32)[:, None] == slot_request[None, :]) & (
        filled[None, :] > 0
    )
    slot_marks = jnp.broadcast_to(
        ((slot_local + 1) * filled).astype(jnp.bfloat16).reshape(peer_count, capacity, 1),
        (peer_count, capacity, Q_LEN),
    )
    first_slot = lax.axis_index("doc") * doc_dev
    owned = doc_slot[None, :] == first_slot + jnp.arange(doc_dev, dtype=jnp.int32)[:, None]
    owned_blocks = jnp.sum(jnp.where(owned, doc_blocks[None, :], 0), axis=1)
    outgoing = jnp.take(
        queries.reshape(requests, Q_LEN, head_count * latent_width), slot_request, axis=0
    )
    payload = lax.all_to_all(
        outgoing.reshape(peer_count, capacity, Q_LEN, head_count * latent_width),
        "doc",
        split_axis=0,
        concat_axis=0,
        tiled=True,
    )
    got_marks = lax.all_to_all(slot_marks, "doc", split_axis=0, concat_axis=0, tiled=True)
    item_count = payload.shape[2]
    slot_queries = payload.reshape(slot_count, item_count, head_count, latent_width)
    answer_item_count = slot_queries.shape[1]
    mark_code = got_marks[:, :, 0].reshape(slot_count).astype(jnp.int32)
    picked = jnp.maximum(mark_code - 1, 0)
    chooser = picked[:, None] == jnp.arange(doc_dev, dtype=jnp.int32)[None, :]
    lengths = jnp.sum(jnp.where(chooser, owned_blocks[None, :], 0), axis=1) * BLOCK
    maxima, totals, normed = slot_partials(slot_queries, full_cache, picked, lengths, w_uv)
    returned = lax.all_to_all(
        normed.reshape(peer_count, capacity, answer_item_count, head_count * VDIM),
        "doc",
        split_axis=0,
        concat_axis=0,
        tiled=True,
    )
    values, maxima, totals = (
        returned,
        lax.all_to_all(
            maxima.reshape(peer_count, capacity, answer_item_count, head_count),
            "doc",
            split_axis=0,
            concat_axis=0,
            tiled=True,
        ),
        lax.all_to_all(
            totals.reshape(peer_count, capacity, answer_item_count, head_count),
            "doc",
            split_axis=0,
            concat_axis=0,
            tiled=True,
        ),
    )
    normed = values.reshape(slot_count, Q_LEN, head_count, VDIM)
    maxima = maxima.reshape(slot_count, Q_LEN, head_count)
    totals = totals.reshape(slot_count, Q_LEN, head_count)
    own_queries = queries.reshape(requests, Q_LEN, head_count, latent_width)
    own_keys = question_latent.reshape(requests, Q_LEN, latent_width)
    places = jnp.arange(Q_LEN, dtype=jnp.int32)
    causal = (places[None, :] <= places[:, None])[None]
    own_max, own_total, own_normed = attend(own_queries, own_keys, causal, w_uv)
    gating = owners[:, :, None, None]
    lifted = jnp.where(gating, maxima[None], LOWEST)
    largest = jnp.maximum(jnp.max(lifted, axis=1), own_max)
    shares = jnp.where(gating, jnp.exp(lifted - largest[:, None]), 0.0) * totals[None]
    own_share = jnp.exp(own_max - largest) * own_total
    denominator = own_share + jnp.sum(shares, axis=1)
    numerator = own_share[..., None] * own_normed.astype(jnp.float32) + jnp.einsum(
        "rsqh,sqhd->rqhd", shares, normed.astype(jnp.float32), precision=lax.Precision.HIGHEST
    )
    result = (numerator / denominator[..., None]).astype(jnp.bfloat16)
    return result.reshape(tokens, head_count * VDIM)


def solution(mesh):
    placed = (
        P("doc", "head"),
        P("doc", "head"),
        P("doc", None),
        P("doc", "head", None),
        P("head", None, None),
        P("head", None, None),
        P(),
        P(),
        P("doc"),
        P("doc"),
    )
    return jax.shard_map(
        on_device, mesh=mesh, in_specs=placed, out_specs=P("doc", "head"), check_vma=False
    )
```

profile of v0, /device:TPU:4, one launch (start us, length us, event | category | flops | bytes accessed | tf_op | source)
XLA Modules:
  0.0 554.2 jit_solution(15189673096598255341)
XLA Ops:
  9.3 11.6 %all-to-all-start = ((bf16[32,2,16]{2,1,0:T(2,128)(2,1)}), bf16[32,2,16]{2,1,0:T(2,128)(2,1)S(1)}, u32[]{:S(2)}, u32[]{:S(2)}) async-start(bf16[32,2,16]{2,1,0:T(2,128)(2,1)} %broadcast_in_dim.205), calls=%async_computation | async-start | bytes 32768 | tf_op jit(solution)/shard_map/all_to_all | solution.py:119
  25.7 2.6 reshape.287
  28.3 6.0 %gather_fusion.1 = bf16[64,16,4608]{2,1,0:T(8,128)(2,1)} fusion(bf16[8,16,4608]{2,1,0:T(8,128)(2,1)S(1)} %reshape.287, s32[1024]{0:T(1024)S(1)} %pad_clamp_fusion.1), kind=kCustom, calls=%fused_computation.1 | custom fusion | bytes 18874624 | tf_op jit(solution)/shard_map/jit(_take)/gather | solution.py:109
  34.2 8.3 %broadcast_select_fusion.1 = bf16[32,2,16,4608]{3,2,1,0:T(8,128)(2,1)} fusion(bf16[32,2,16,4608]{3,2,1,0:T(8,128)(2,1)} %bitcast.140, pred[32,2]{1,0:T(8,128)(4,1)S(1)} %compare_and_fusion.1), kind=kLoop, calls=%fused_computation.35 | loop fusion | flops 4718592 | bytes 18874432 | tf_op jit(solution)/shard_map/jit(_take)/select_n | solution.py:109
  42.5 10.0 %all-to-all-start.1 = ((bf16[32,2,16,4608]{3,2,1,0:T(8,128)(2,1)}), bf16[32,2,16,4608]{3,2,1,0:T(8,128)(2,1)}, u32[]{:S(2)}, u32[]{:S(2)}) async-start(bf16[32,2,16,4608]{3,2,1,0:T(8,128)(2,1)} %broadcast_select_fusion.1), calls=%async_computation.1 | async-start | bytes 18874368 | tf_op jit(solution)/shard_map/all_to_all | solution.py:112
  54.5 206.2 %all-to-all-done.1 = bf16[32,2,16,4608]{3,2,1,0:T(8,128)(2,1)} async-done(((bf16[32,2,16,4608]{3,2,1,0:T(8,128)(2,1)}), bf16[32,2,16,4608]{3,2,1,0:T(8,128)(2,1)}, u32[]{:S(2)}, u32[]{:S(2)}) %all-to-all-start.1) | async-done | bytes 9437216 | tf_op jit(solution)/shard_map/all_to_all | solution.py:112
  260.7 17.7 %reshape_reshape.12 = bf16[8,8,16,8,576]{4,3,2,1,0:T(8,128)(2,1)} reshape(bf16[32,2,16,4608]{3,2,1,0:T(8,128)(2,1)} %all-to-all-done.1) | data formatting | bytes 18874368 | tf_op jit(solution)/shard_map/reshape;reshape | solution.py:50
  278.4 164.7 %while.15 = (s32[]{:T(128)}, f32[8,8,16,8]{2,3,1,0:T(8,128)S(1)}, f32[8,8,16,8]{2,3,1,0:T(8,128)S(1)}, bf16[8,8,16,8,128]{4,3,2,1,0:T(8,128)(2,1)}, s32[8,8]{1,0...) while((s32[]{:T(128)}, f32[8,8,16,8]{2,3,1,0:T(8,128)S(1)}, ...), condition=%wide.region_11.12_spmd.clone, body=%wide.region_8.11_spmd.clone.sunk | while | flops 1282935808 | bytes 56288672 | solution.py:54
  278.5 7.5 %gather_fusion = bf16[8,512,576]{2,1,0:T(8,128)(2,1)} fusion(bf16[16,512,576]{2,1,0:T(8,128)(2,1)} %get-tuple-element.229, s32[1024]{0:T(1024)S(1)} %pad_clamp_fusion.3), kind=kCustom, calls=%fused_computation.clone.clone.1 | custom fusion | bytes 9437216 | tf_op jit(solution)/shard_map/while/body/eval_jaxpr/jit(_take)/gather | solution.py:45
  286.0 3.1 broadcast_select_fusion.3
  289.2 4.2 fusion.83
  294.2 3.7 fusion.85
  299.0 7.5 %gather_fusion = bf16[8,512,576]{2,1,0:T(8,128)(2,1)} fusion(bf16[16,512,576]{2,1,0:T(8,128)(2,1)} %get-tuple-element.229, s32[1024]{0:T(1024)S(1)} %pad_clamp_fusion.3), kind=kCustom, calls=%fused_computation.clone.clone.1 | custom fusion | bytes 9437216 | tf_op jit(solution)/shard_map/while/body/eval_jaxpr/jit(_take)/gather | solution.py:45
  306.5 3.1 broadcast_select_fusion.3
  309.7 4.2 fusion.83
  314.8 3.7 fusion.85
  319.6 7.5 %gather_fusion = bf16[8,512,576]{2,1,0:T(8,128)(2,1)} fusion(bf16[16,512,576]{2,1,0:T(8,128)(2,1)} %get-tuple-element.229, s32[1024]{0:T(1024)S(1)} %pad_clamp_fusion.3), kind=kCustom, calls=%fused_computation.clone.clone.1 | custom fusion | bytes 9437216 | tf_op jit(solution)/shard_map/while/body/eval_jaxpr/jit(_take)/gather | solution.py:45
  327.1 3.1 broadcast_select_fusion.3
  330.3 4.2 fusion.83
  335.4 3.7 fusion.85
  340.2 7.5 %gather_fusion = bf16[8,512,576]{2,1,0:T(8,128)(2,1)} fusion(bf16[16,512,576]{2,1,0:T(8,128)(2,1)} %get-tuple-element.229, s32[1024]{0:T(1024)S(1)} %pad_clamp_fusion.3), kind=kCustom, calls=%fused_computation.clone.clone.1 | custom fusion | bytes 9437216 | tf_op jit(solution)/shard_map/while/body/eval_jaxpr/jit(_take)/gather | solution.py:45
  347.7 3.1 broadcast_select_fusion.3
  350.9 4.2 fusion.83
  356.0 3.7 fusion.85
  360.8 7.5 %gather_fusion = bf16[8,512,576]{2,1,0:T(8,128)(2,1)} fusion(bf16[16,512,576]{2,1,0:T(8,128)(2,1)} %get-tuple-element.229, s32[1024]{0:T(1024)S(1)} %pad_clamp_fusion.3), kind=kCustom, calls=%fused_computation.clone.clone.1 | custom fusion | bytes 9437216 | tf_op jit(solution)/shard_map/while/body/eval_jaxpr/jit(_take)/gather | solution.py:45
  368.3 3.1 broadcast_select_fusion.3
  371.5 4.2 fusion.83
  376.6 3.7 fusion.85
  381.4 7.5 %gather_fusion = bf16[8,512,576]{2,1,0:T(8,128)(2,1)} fusion(bf16[16,512,576]{2,1,0:T(8,128)(2,1)} %get-tuple-element.229, s32[1024]{0:T(1024)S(1)} %pad_clamp_fusion.3), kind=kCustom, calls=%fused_computation.clone.clone.1 | custom fusion | bytes 9437216 | tf_op jit(solution)/shard_map/while/body/eval_jaxpr/jit(_take)/gather | solution.py:45
  388.9 3.1 broadcast_select_fusion.3
  392.1 4.2 fusion.83
  397.2 3.7 fusion.85
  402.0 7.5 %gather_fusion = bf16[8,512,576]{2,1,0:T(8,128)(2,1)} fusion(bf16[16,512,576]{2,1,0:T(8,128)(2,1)} %get-tuple-element.229, s32[1024]{0:T(1024)S(1)} %pad_clamp_fusion.3), kind=kCustom, calls=%fused_computation.clone.clone.1 | custom fusion | bytes 9437216 | tf_op jit(solution)/shard_map/while/body/eval_jaxpr/jit(_take)/gather | solution.py:45
  409.5 3.1 broadcast_select_fusion.3
  412.7 4.2 fusion.83
  417.8 3.7 fusion.85
  422.6 7.5 %gather_fusion = bf16[8,512,576]{2,1,0:T(8,128)(2,1)} fusion(bf16[16,512,576]{2,1,0:T(8,128)(2,1)} %get-tuple-element.229, s32[1024]{0:T(1024)S(1)} %pad_clamp_fusion.3), kind=kCustom, calls=%fused_computation.clone.clone.1 | custom fusion | bytes 9437216 | tf_op jit(solution)/shard_map/while/body/eval_jaxpr/jit(_take)/gather | solution.py:45
  430.1 3.1 broadcast_select_fusion.3
  433.3 4.2 fusion.83
  438.4 3.7 fusion.85
  443.9 19.3 %all-to-all-start.2 = ((f32[32,1,256]{2,1,0:T(1,128)}), f32[32,1,256]{2,1,0:T(1,128)S(1)}, u32[]{:S(2)}, u32[]{:S(2)}) async-start(f32[32,1,256]{2,1,0:T(1,128)} %reshape.319), calls=%async_computation.2 | async-start | bytes 65536 | tf_op jit(solution)/shard_map/all_to_all | solution.py:137
  464.0 7.1 %all-to-all-done.2 = f32[32,1,256]{2,1,0:T(1,128)S(1)} async-done(((f32[32,1,256]{2,1,0:T(1,128)}), f32[32,1,256]{2,1,0:T(1,128)S(1)}, u32[]{:S(2)}, u32[]{:S(2)}) %all-to-all-start.2) | async-done | bytes 32800 | tf_op jit(solution)/shard_map/all_to_all | solution.py:137
  471.0 5.7 %all-to-all-start.4 = ((f32[32,1,256]{2,1,0:T(1,128)}), f32[32,1,256]{2,1,0:T(1,128)S(1)}, u32[]{:S(2)}, u32[]{:S(2)}) async-start(f32[32,1,256]{2,1,0:T(1,128)} %reshape.317), calls=%async_computation.4 | async-start | bytes 65536 | tf_op jit(solution)/shard_map/all_to_all | solution.py:144
  476.8 4.2 reshape_reshape.14
  481.0 3.8 all-to-all-done.4
  484.7 6.5 %all-to-all-start.3 = ((bf16[32,2,16,1024]{3,2,1,0:T(8,128)(2,1)}), bf16[32,2,16,1024]{3,2,1,0:T(8,128)(2,1)}, u32[]{:S(2)}, u32[]{:S(2)}) async-start(bf16[32,2,16,1024]{3,2,1,0:T(8,128)(2,1)} %reshape_reshape.14), calls=%async_computation.3 | async-start | bytes 4194304 | tf_op jit(solution)/shard_map/all_to_all | solution.py:128
  497.3 41.0 %all-to-all-done.3 = bf16[32,2,16,1024]{3,2,1,0:T(8,128)(2,1)} async-done(((bf16[32,2,16,1024]{3,2,1,0:T(8,128)(2,1)}), bf16[32,2,16,1024]{3,2,1,0:T(8,128)(2,1)}, u32[]{:S(2)}, u32[]{:S(2)}) %all-to-all-start.3) | async-done | bytes 2097184 | tf_op jit(solution)/shard_map/all_to_all | solution.py:128
  540.5 3.8 fusion.21
  (182 shorter events, 37.9 us)
Async XLA Ops:
  6.5 15.5 %copy-start = (bf16[8,128,512]{2,1,0:T(8,128)(2,1)S(1)}, bf16[8,128,512]{2,1,0:T(8,128)(2,1)}, u32[]{:S(2)}) copy-start(bf16[8,128,512]{2,1,0:T(8,128)(2,1)} %param.16) | copy-start | bytes 3145732
  9.3 33.2 %all-to-all-start = ((bf16[32,2,16]{2,1,0:T(2,128)(2,1)}), bf16[32,2,16]{2,1,0:T(2,128)(2,1)S(1)}, u32[]{:S(2)}, u32[]{:S(2)}) async-start(bf16[32,2,16]{2,1,0:T(2,128)(2,1)} %broadcast_in_dim.205), calls=%async_computation | async-start | bytes 32768 | tf_op jit(solution)/shard_map/all_to_all | solution.py:119
  42.5 10.8 %copy-start.5 = (s32[512]{0:T(512)S(1)}, s32[512]{0:T(512)}, u32[]{:S(2)}) copy-start(s32[512]{0:T(512)} %param.18) | copy-start | bytes 6148
  42.5 10.8 %copy-start.6 = (s32[512]{0:T(512)S(1)}, s32[512]{0:T(512)}, u32[]{:S(2)}) copy-start(s32[512]{0:T(512)} %param.19) | copy-start | bytes 6148
  42.5 218.2 %all-to-all-start.1 = ((bf16[32,2,16,4608]{3,2,1,0:T(8,128)(2,1)}), bf16[32,2,16,4608]{3,2,1,0:T(8,128)(2,1)}, u32[]{:S(2)}, u32[]{:S(2)}) async-start(bf16[32,2,16,4608]{3,2,1,0:T(8,128)(2,1)} %broadcast_select_fusion.1), calls=%async_computation.1 | async-start | bytes 18874368 | tf_op jit(solution)/shard_map/all_to_all | solution.py:112
  52.5 225.9 %all-gather.2.cloned.1.call-start = ((), (), s32[]{:S(2)}) async-start(), calls=%async_computation.5 | async-start | bytes 11796480 | tf_op jit(solution)/shard_map/all_gather | solution.py:81
  289.1 4.3 copy-start.2
  309.6 4.3 copy-start.2
  330.2 4.3 copy-start.2
  350.8 4.3 copy-start.2
  371.4 4.3 copy-start.2
  392.0 4.3 copy-start.2
  412.6 4.3 copy-start.2
  433.2 4.3 copy-start.2
  443.9 27.1 %all-to-all-start.2 = ((f32[32,1,256]{2,1,0:T(1,128)}), f32[32,1,256]{2,1,0:T(1,128)S(1)}, u32[]{:S(2)}, u32[]{:S(2)}) async-start(f32[32,1,256]{2,1,0:T(1,128)} %reshape.319), calls=%async_computation.2 | async-start | bytes 65536 | tf_op jit(solution)/shard_map/all_to_all | solution.py:137
  471.0 13.7 %all-to-all-start.4 = ((f32[32,1,256]{2,1,0:T(1,128)}), f32[32,1,256]{2,1,0:T(1,128)S(1)}, u32[]{:S(2)}, u32[]{:S(2)}) async-start(f32[32,1,256]{2,1,0:T(1,128)} %reshape.317), calls=%async_computation.4 | async-start | bytes 65536 | tf_op jit(solution)/shard_map/all_to_all | solution.py:144
  484.7 53.6 %all-to-all-start.3 = ((bf16[32,2,16,1024]{3,2,1,0:T(8,128)(2,1)}), bf16[32,2,16,1024]{3,2,1,0:T(8,128)(2,1)}, u32[]{:S(2)}, u32[]{:S(2)}) async-start(bf16[32,2,16,1024]{3,2,1,0:T(8,128)(2,1)} %reshape_reshape.14), calls=%async_computation.3 | async-start | bytes 4194304 | tf_op jit(solution)/shard_map/all_to_all | solution.py:128
  491.3 0.9 copy-start.3
  491.3 1.1 copy-start.4
  540.5 3.9 copy-start.7
  544.4 3.0 copy-start.1
Sparse Core Ops, SparseCore 0:
  55.2 62.1 all-gather.1
where the time goes:
time: 556 us; the launch traced here: 554 us
  waiting for transfers between devices  259 us (47%)
  local copies, waits for them, and re-layouts  111 us (20%)
  matrix products  71.4 us (13%)
  starting transfers between devices  53.2 us (10%)
  other arithmetic  45.2 us (8%)
  between operations  13.8 us (2%)
    all_to_all x1, waiting for transfers between devices, on_device(): lax.all_to_all(outgoing.reshape(peer_count, capacity, Q_LEN, head_count *...  206 us
    gather x8, local copies, waits for them, and re-layouts, one_block(): key_rows = jnp.take(table, block_picked, axis=0)  60 us
    all_to_all x1, waiting for transfers between devices, on_device(): lax.all_to_all(normed.reshape(peer_count, capacity, answer_item_count, he...  41 us
    dot_general x9, matrix products, attend(): jnp.einsum('bqhc,blc->bqhl', queries, key_rows, preferred_element_type=jn...  34.2 us
    dot_general x9, matrix products, attend(): jnp.einsum('bqhc,hcd->bqhd', latent, w_uv, preferred_element_type=jnp.flo...  31.9 us
    select_n x16, other arithmetic, one_block(): key_rows = jnp.take(table, block_picked, axis=0)  24.8 us
    all_to_all x1, starting transfers between devices, on_device(): lax.all_to_all(maxima.reshape(peer_count, capacity, answer_item_count, he...  19.3 us
    another operation x1, local copies, waits for them, and re-layouts, slot_partials(): queries.reshape((blocks, slot_group) + queries.shape[1:])  17.7 us
  transfers between devices with their start and end apart: 6, of which 4 were waited for; matrix products, arithmetic and copies ran while one was open for 9% of the time, Pallas kernels for 0%

commit v1 on v0

v1 whole, which is shorter than its diff:
```python
import functools

import jax
import jax.numpy as jnp
from jax import lax
from jax.experimental import pallas as pl
from jax.experimental.pallas import tpu as pltpu
from jax.sharding import PartitionSpec as P

RANK = 512
ROPE = 64
NOPE = 128
VDIM = 128
LATENT = RANK + ROPE
Q_LEN = 16
BLOCK = 128
NBLK = 4
HD = 8
TOK = 128
REQ = 8
DOC_DEV = 16
PAIRS = 32
CAP = 2
ROWS = CAP * Q_LEN
NX, NZ, NY = 4, 8, 4
N_DOC = NX * NZ
SLOTS = N_DOC * CAP
QW = HD * (NOPE + ROPE)
VW = HD * VDIM
POS = 64
SCALE = (NOPE + ROPE) ** (-0.5)
LOWEST = -1e30
MESH = pl.DeviceIdType.MESH
F32 = jnp.float32
BF16 = jnp.bfloat16
VMEM_LIMIT = 56 * 1024 * 1024


def dot(a, b, dims):
    return lax.dot_general(a, b, (dims, ((), ())), preferred_element_type=F32)


def greet(peers):
    barrier = pltpu.get_barrier_semaphore()
    for peer in peers:
        pl.semaphore_signal(barrier, inc=1, device_id=peer, device_id_type=MESH)
    pl.semaphore_wait(barrier, len(peers))


def spread_kernel(
    q_ref, tbl_ref, doc_ref, slots_ref, tblout_ref, full_ref,
    gq, sendb, tblb, zs, zr, ts, tr, us, ur, xs, xr, ys, yr, cs, cr, ls,
):
    d = lax.axis_index("doc")
    h = lax.axis_index("head")
    z, x = d // NX, d % NX
    y, c = h // 2, h % 2
    right = (((z + 1) % NZ) * NX + x, h)
    left = (((z + NZ - 1) % NZ) * NX + x, h)
    z_peer = [None] + [(((z + j) % NZ) * NX + x, h) for j in range(1, NZ)]
    x_peer = [None] + [(z * NX + (x + j) % NX, h) for j in range(1, NX)]
    h_up = ((y + 1) % NY) * 2 + c
    h_down = ((y + NY - 1) % NY) * 2 + c
    h_far = ((y + 2) % NY) * 2 + c
    up, down, other = (d, h_up), (d, h_down), (d, y * 2 + 1 - c)
    greet(z_peer[1:] + x_peer[1:] + [up, down, other])

    def remote(src, dst, send, recv, peer):
        return pltpu.make_async_remote_copy(
            src_ref=src, dst_ref=dst, send_sem=send, recv_sem=recv, device_id=peer, device_id_type=MESH
        )

    def ring(i, src, dst, peer):
        return remote(src, dst, zs.at[i], zr.at[i], peer)

    half = TOK // 2
    low, high = pl.ds(0, half), pl.ds(half, half)
    ring_copies = [
        ring(0, q_ref, gq.at[7], right),
        ring(1, q_ref, gq.at[1], left),
        ring(2, gq.at[7], gq.at[6], right),
        ring(3, gq.at[1], gq.at[2], left),
        ring(4, gq.at[6], gq.at[5], right),
        ring(5, gq.at[2], gq.at[3], left),
        ring(6, gq.at[5, low], gq.at[4, low], right),
        ring(7, gq.at[3, high], gq.at[4, high], left),
    ]
    ring_copies[0].start()
    ring_copies[1].start()

    tables = [
        remote(tbl_ref.at[(z + j) % NZ], tblb.at[z], ts.at[j], tr.at[j], z_peer[j]) for j in range(1, NZ)
    ]
    for copy in tables:
        copy.start()

    def place(head):
        return full_ref.at[:, pl.ds(pl.multiple_of(head * POS, POS), POS), :]

    def part(head, first):
        return full_ref.at[
            pl.ds(first, DOC_DEV // 2), pl.ds(pl.multiple_of(head * POS, POS), POS), :
        ]

    own_docs = pltpu.make_async_copy(doc_ref, place(h), ls.at[0])
    docs_up = remote(doc_ref, place(h), ys.at[0], yr.at[0], up)
    docs_down = remote(doc_ref, place(h), ys.at[1], yr.at[1], down)
    docs_other = remote(doc_ref, place(h), cs.at[0], cr.at[0], other)
    docs_up.start()
    docs_down.start()
    docs_other.start()
    own_docs.start()

    tblb[pl.ds(z, 1)] = tbl_ref[pl.ds(z, 1)]
    for copy in tables:
        copy.wait_recv()
    passed = [
        remote(tblb, tblout_ref.at[x], us.at[j], ur.at[j], x_peer[j]) for j in range(1, NX)
    ]
    for copy in passed:
        copy.start()
    own_table = pltpu.make_async_copy(tblb, tblout_ref.at[x], ls.at[1])
    own_table.start()

    token = lax.broadcasted_iota(jnp.int32, (TOK, NX * ROWS), 0)
    pending = []

    def forward(rel):
        owner = (z + rel) % NZ
        wanted = tblb[owner][:, 0:TOK]
        pick = jnp.where(token == wanted, 1.0, 0.0).astype(BF16)
        source = q_ref if rel == 0 else gq.at[rel]
        for k in range(0, QW, 512):
            chosen = dot(pick, source[:, k : k + 512], ((0,), (0,))).astype(BF16)
            sendb[rel, :, :, k : k + 512] = chosen.reshape(NX, ROWS, 512)
        target = slots_ref.at[owner * NX + x]
        for j in range(1, NX):
            copy = remote(
                sendb.at[rel, (x + j) % NX], target, xs.at[rel, j], xr.at[rel, j], x_peer[j]
            )
            copy.start()
            pending.append(copy)
        copy = pltpu.make_async_copy(sendb.at[rel, x], target, ls.at[2 + rel])
        copy.start()
        kept.append(copy)

    kept = [own_docs, own_table]
    forward(0)
    for i, (a, b) in enumerate(((7, 1), (6, 2), (5, 3))):
        ring_copies[2 * i].wait_recv()
        ring_copies[2 * i + 2].start()
        ring_copies[2 * i + 1].wait_recv()
        ring_copies[2 * i + 3].start()
        forward(a)
        forward(b)

    docs_up.wait_recv()
    pass_up = remote(part(h_down, 0), part(h_down, 0), ys.at[2], yr.at[2], up)
    pass_up.start()
    cross_down = remote(place(h_down), place(h_down), cs.at[1], cr.at[1], other)
    cross_down.start()
    docs_down.wait_recv()
    pass_down = remote(part(h_up, 8), part(h_up, 8), ys.at[3], yr.at[3], down)
    pass_down.start()
    cross_up = remote(place(h_up), place(h_up), cs.at[2], cr.at[2], other)
    cross_up.start()

    ring_copies[6].wait_recv()
    ring_copies[7].wait_recv()
    forward(4)

    pass_up.wait_recv()
    pass_down.wait_recv()
    cross_far = remote(place(h_far), place(h_far), cs.at[3], cr.at[3], other)
    cross_far.start()

    for copy in pending + passed + [docs_other, cross_down, cross_up, cross_far]:
        copy.wait_recv()
    for copy in kept:
        copy.wait()
    for copy in (
        ring_copies + tables + passed + pending
        + [docs_up, docs_down, docs_other, pass_up, pass_down, cross_down, cross_up, cross_far]
    ):
        copy.wait_send()


def spread(q, table, doc_cache):
    anywhere = pl.BlockSpec(memory_space=pl.ANY)
    local = pl.BlockSpec(memory_space=pltpu.VMEM)
    dma = pltpu.SemaphoreType.DMA
    return pl.pallas_call(
        spread_kernel,
        out_shape=(
            jax.ShapeDtypeStruct((N_DOC, ROWS, QW), BF16),
            jax.ShapeDtypeStruct((NX, NZ, 1, 256), jnp.int32),
            jax.ShapeDtypeStruct((DOC_DEV, NBLK * BLOCK, LATENT), BF16),
        ),
        in_specs=[local, local, anywhere],
        out_specs=(anywhere, anywhere, anywhere),
        scratch_shapes=[
            pltpu.VMEM((NZ, TOK, QW), BF16),
            pltpu.VMEM((NZ, NX, ROWS, QW), BF16),
            pltpu.VMEM((NZ, 1, 256), jnp.int32),
            dma((8,)), dma((8,)),
            dma((NZ,)), dma((NZ,)),
            dma((NX,)), dma((NX,)),
            dma((NZ, NX)), dma((NZ, NX)),
            dma((4,)), dma((4,)),
            dma((4,)), dma((4,)),
            dma((10,)),
        ],
        compiler_params=pltpu.CompilerParams(
            collective_id=0, has_side_effects=True, vmem_limit_bytes=VMEM_LIMIT
        ),
        name="spread",
    )(q, table, doc_cache)


def softmax_rows(scores):
    largest = jnp.max(scores, axis=1, keepdims=True)
    weights = jnp.exp((scores - largest) * SCALE)
    totals = jnp.sum(weights, axis=1, keepdims=True)
    return weights.astype(BF16), totals, largest * SCALE + jnp.log(totals)


def attend_kernel(
    code_ref, blk_ref, slots_ref, full_ref, uk_ref, uv_ref, out_ref, lse_ref, qa, qr
):
    for head in range(HD):
        nope = slots_ref[:, :, head * NOPE : (head + 1) * NOPE].reshape(SLOTS * Q_LEN, NOPE)
        absorbed = dot(nope, uk_ref[head], ((1,), (0,))).astype(BF16)
        qa[:, head] = absorbed.reshape(SLOTS, Q_LEN, RANK)
        first = HD * NOPE + head * ROPE
        rope = slots_ref[:, :, first : first + ROPE].reshape(SLOTS, Q_LEN, ROPE)
        qr[:, head] = rope

    row = lax.broadcasted_iota(jnp.int32, (TOK, TOK), 0)
    column = lax.broadcasted_iota(jnp.int32, (TOK, TOK), 1)
    diagonal = row == column

    def one_slot(s, carry):
        blocks = blk_ref[s]
        doc = code_ref[s]
        for count in range(1, NBLK + 1):

            @pl.when(blocks == count)
            def _():
                length = count * BLOCK
                latent_q = qa[s].reshape(HD * Q_LEN, RANK)
                rope_q = qr[s].reshape(HD * Q_LEN, ROPE)
                keys = full_ref[doc, 0:length, 0:RANK]
                rope_k = full_ref[doc, 0:length, RANK:LATENT]
                scores = dot(latent_q, keys, ((1,), (1,))) + dot(rope_q, rope_k, ((1,), (1,)))
                weights, totals, lse = softmax_rows(scores)
                latent = dot(weights, keys, ((1,), (0,))) / totals
                qa[s] = latent.astype(BF16).reshape(HD, Q_LEN, RANK)
                lse_ref[s] = jnp.sum(jnp.where(diagonal, lse, 0.0), axis=0, keepdims=True)

        return carry

    lax.fori_loop(0, SLOTS, one_slot, 0)

    for head in range(HD):
        latent = qa[:, head].reshape(SLOTS * Q_LEN, RANK)
        values = dot(latent, uv_ref[head], ((1,), (0,))).astype(BF16)
        out_ref[:, :, head * VDIM : (head + 1) * VDIM] = values.reshape(N_DOC, ROWS, VDIM)


def attend(code, blocks, slots, full_cache, w_uk, w_uv):
    smem = pl.BlockSpec(memory_space=pltpu.SMEM)
    local = pl.BlockSpec(memory_space=pltpu.VMEM)
    return pl.pallas_call(
        attend_kernel,
        out_shape=(
            jax.ShapeDtypeStruct((N_DOC, ROWS, VW), BF16),
            jax.ShapeDtypeStruct((SLOTS, 1, TOK), F32),
        ),
        in_specs=[smem, smem, local, local, local, local],
        out_specs=(local, local),
        scratch_shapes=[
            pltpu.VMEM((SLOTS, HD, Q_LEN, RANK), BF16),
            pltpu.VMEM((SLOTS, HD, Q_LEN, ROPE), BF16),
        ],
        compiler_params=pltpu.CompilerParams(vmem_limit_bytes=VMEM_LIMIT),
        name="attend",
    )(code, blocks, slots, full_cache, w_uk, w_uv)


def give_back_kernel(val_ref, lse_ref, val_out, lse_out, vs, vr, es, er, ls):
    d = lax.axis_index("doc")
    h = lax.axis_index("head")
    barrier = pltpu.get_barrier_semaphore()

    def hello(j, carry):
        pl.semaphore_signal(barrier, inc=1, device_id=((d + j) % N_DOC, h), device_id_type=MESH)
        return carry

    lax.fori_loop(1, N_DOC, hello, 0)
    pl.semaphore_wait(barrier, N_DOC - 1)

    def copies(j):
        peer = (d + j) % N_DOC
        return [
            pltpu.make_async_remote_copy(
                src_ref=src.at[peer], dst_ref=dst.at[d], send_sem=send.at[j], recv_sem=recv.at[j],
                device_id=(peer, h), device_id_type=MESH,
            )
            for src, dst, send, recv in ((val_ref, val_out, vs, vr), (lse_ref, lse_out, es, er))
        ]

    def begin(j, carry):
        for copy in copies(j):
            copy.start()
        return carry

    def end(j, carry):
        for copy in copies(j):
            copy.wait()
        return carry

    lax.fori_loop(1, N_DOC, begin, 0)
    kept = [
        pltpu.make_async_copy(val_ref.at[d], val_out.at[d], ls.at[0]),
        pltpu.make_async_copy(lse_ref.at[d], lse_out.at[d], ls.at[1]),
    ]
    for copy in kept:
        copy.start()
    lax.fori_loop(1, N_DOC, end, 0)
    for copy in kept:
        copy.wait()


def give_back(values, lse):
    anywhere = pl.BlockSpec(memory_space=pl.ANY)
    dma = pltpu.SemaphoreType.DMA
    return pl.pallas_call(
        give_back_kernel,
        out_shape=(
            jax.ShapeDtypeStruct(values.shape, BF16),
            jax.ShapeDtypeStruct(lse.shape, F32),
        ),
        in_specs=[anywhere, anywhere],
        out_specs=(anywhere, anywhere),
        scratch_shapes=[dma((N_DOC,)), dma((N_DOC,)), dma((N_DOC,)), dma((N_DOC,)), dma((2,))],
        compiler_params=pltpu.CompilerParams(collective_id=1, has_side_effects=True),
        name="give_back",
    )(values, lse)


def merge_kernel(
    pos_ref, req_ref, q_ref, ql_ref, uk_ref, uv_ref, val_ref, lse_ref, out_ref, top, den, acc
):
    row = lax.broadcasted_iota(jnp.int32, (TOK, TOK), 0)
    column = lax.broadcasted_iota(jnp.int32, (TOK, TOK), 1)
    visible = (row // Q_LEN == column // Q_LEN) & (column <= row)
    diagonal = row == column
    keys = ql_ref[:, 0:RANK]
    rope_k = ql_ref[:, RANK:LATENT]
    for head in range(HD):
        nope = q_ref[:, head * NOPE : (head + 1) * NOPE]
        first = HD * NOPE + head * ROPE
        absorbed = dot(nope, uk_ref[head], ((1,), (0,))).astype(BF16)
        scores = dot(absorbed, keys, ((1,), (1,))) + dot(
            q_ref[:, first : first + ROPE], rope_k, ((1,), (1,))
        )
        weights, totals, lse = softmax_rows(jnp.where(visible, scores, LOWEST))
        latent = (dot(weights, keys, ((1,), (0,))) / totals).astype(BF16)
        values = dot(latent, uv_ref[head], ((1,), (0,))).astype(BF16).astype(F32)
        acc[:, head] = values.reshape(REQ, Q_LEN, VDIM)
        top[:, head] = jnp.broadcast_to(lse, (TOK, VDIM)).reshape(REQ, Q_LEN, VDIM)
    den[...] = jnp.ones_like(den)

    def one_pair(k, carry):
        slot = pos_ref[k]
        request = req_ref[k]
        lse = jnp.sum(jnp.where(diagonal, lse_ref[slot], 0.0), axis=1, keepdims=True)
        lse = jnp.broadcast_to(lse, (TOK, VDIM)).reshape(HD, Q_LEN, VDIM)
        values = val_ref[slot]
        for head in range(HD):
            old = top[request, head]
            new = jnp.maximum(old, lse[head])
            keep = jnp.exp(old - new)
            fresh = jnp.exp(lse[head] - new)
            part = values[:, head * VDIM : (head + 1) * VDIM].astype(F32)
            top[request, head] = new
            den[request, head] = den[request, head] * keep + fresh
            acc[request, head] = acc[request, head] * keep + fresh * part
        return carry

    lax.fori_loop(0, PAIRS, one_pair, 0)
    for head in range(HD):
        result = (acc[:, head] / den[:, head]).astype(BF16)
        out_ref[:, head * VDIM : (head + 1) * VDIM] = result.reshape(TOK, VDIM)


def merge(position, request, q, question_latent, w_uk, w_uv, values, lse):
    smem = pl.BlockSpec(memory_space=pltpu.SMEM)
    local = pl.BlockSpec(memory_space=pltpu.VMEM)
    return pl.pallas_call(
        merge_kernel,
        out_shape=jax.ShapeDtypeStruct((TOK, VW), BF16),
        in_specs=[smem, smem] + [local] * 6,
        out_specs=local,
        scratch_shapes=[pltpu.VMEM((REQ, HD, Q_LEN, VDIM), F32)] * 3,
        compiler_params=pltpu.CompilerParams(vmem_limit_bytes=VMEM_LIMIT),
        name="merge",
    )(position, request, q, question_latent, w_uk, w_uv, values, lse)


def on_device(
    q_nope, q_rope, question_latent, doc_cache, w_uk, w_uv, doc_slot, doc_blocks, pair_doc, pair_req
):
    device = lax.axis_index("doc")
    q = jnp.concatenate([q_nope, q_rope], axis=1)
    doc_ids = jnp.arange(doc_slot.shape[0], dtype=jnp.int32)
    matches = pair_doc[:, None] == doc_ids[None, :]
    pair_slot = jnp.sum(jnp.where(matches, doc_slot[None, :], 0), axis=1)
    target = pair_slot // DOC_DEV
    sequence = jnp.arange(PAIRS, dtype=jnp.int32)
    before = (target[:, None] == target[None, :]) & (sequence[None, :] < sequence[:, None])
    position = target * CAP + jnp.sum(before.astype(jnp.int32), axis=1)
    placed = jnp.arange(SLOTS, dtype=jnp.int32)[:, None] == position[None, :]
    first_token = jnp.sum(jnp.where(placed, pair_req[None, :] * Q_LEN + 1, 0), axis=1) - 1
    code = jnp.sum(jnp.where(placed, pair_slot[None, :] % DOC_DEV + 1, 0), axis=1)
    tokens = jnp.where(
        first_token[:, None] >= 0, first_token[:, None] + jnp.arange(Q_LEN, dtype=jnp.int32), -1
    )
    table = jnp.concatenate(
        [
            tokens.reshape(NZ, 1, NX * ROWS),
            jnp.broadcast_to(code[:, None], (SLOTS, Q_LEN)).reshape(NZ, 1, NX * ROWS),
        ],
        axis=2,
    )
    owned = doc_slot[None, :] == device * DOC_DEV + jnp.arange(DOC_DEV, dtype=jnp.int32)[:, None]
    owned_blocks = jnp.sum(jnp.where(owned, doc_blocks[None, :], 0), axis=1)

    slots, tables, full_cache = spread(q, table, doc_cache)

    got = tables.reshape(NX, NZ, 2, NX, CAP, Q_LEN)[:, :, 1, :, :, 0]
    mine = jnp.arange(NX, dtype=jnp.int32) == device % NX
    got = jnp.sum(jnp.where(mine[None, None, :, None], got, 0), axis=2)
    got = got.transpose(1, 0, 2).reshape(SLOTS)
    chooser = got[:, None] == jnp.arange(1, DOC_DEV + 1, dtype=jnp.int32)[None, :]
    blocks = jnp.sum(jnp.where(chooser, owned_blocks[None, :], 0), axis=1)
    values, lse = attend(jnp.maximum(got - 1, 0), blocks, slots, full_cache, w_uk, w_uv)
    values, lse = give_back(values, lse.reshape(N_DOC, CAP, TOK))
    return merge(
        position, pair_req, q, question_latent, w_uk, w_uv,
        values.reshape(SLOTS, Q_LEN, VW), lse.reshape(SLOTS, 1, TOK),
    )


def solution(mesh):
    placed = (
        P("doc", "head"),
        P("doc", "head"),
        P("doc", None),
        P("doc", "head", None),
        P("head", None, None),
        P("head", None, None),
        P(),
        P(),
        P("doc"),
        P("doc"),
    )
    return jax.shard_map(
        on_device, mesh=mesh, in_specs=placed, out_specs=P("doc", "head"), check_vma=False
    )
```

time: 556 us -> 182 us (0.33)
  waiting for transfers between devices: 259 us -> 0 us
  Pallas kernels: 0 us -> 172 us
  local copies, waits for them, and re-layouts: 111 us -> 5.08 us
  matrix products: 71.4 us -> 0 us
  starting transfers between devices: 53.2 us -> 0 us
  other arithmetic: 45.2 us -> 4.83 us
  between operations: 13.8 us -> 0.15 us
    all_to_all x5 -> x0, waiting for transfers between devices: 258 us -> none  [the longest x1 206 us: on_device(): lax.all_to_all(outgoing.reshape(peer_count, capacity, Q_LEN, head_count *...]
    pallas_call x0 -> x4, Pallas kernels: none -> 172 us  [the longest x1 60.9 us: give_back(): pl.pallas_call(give_back_kernel, out_shape=(jax.ShapeDtypeStruct(values.s...]
    dot_general x20 -> x0, matrix products: 71.4 us -> none  [the longest x9 34.2 us: attend(): jnp.einsum('bqhc,blc->bqhl', queries, key_rows, preferred_element_type=jn...]
    gather x9 -> x0, local copies, waits for them, and re-layouts: 66 us -> none  [the longest x8 60 us: one_block(): key_rows = jnp.take(table, block_picked, axis=0)]
    all_to_all x5 -> x0, starting transfers between devices: 53.1 us -> none  [the longest x1 19.3 us: on_device(): lax.all_to_all(maxima.reshape(peer_count, capacity, answer_item_count, he...]
    select_n x19 -> x1, other arithmetic: 33.1 us -> 0.01 us  [on_device(): jnp.where(first_token[:, None] >= 0, first_token[:, None] + jnp.arange(Q_...]
    another operation x2 -> x0, local copies, waits for them, and re-layouts: 21.9 us -> none  [the longest x1 17.7 us: slot_partials(): queries.reshape((blocks, slot_group) + queries.shape[1:])]
    dynamic_update_slice x32 -> x0, local copies, waits for them, and re-layouts: 8.37 us -> none  [slot_partials(): maxima, totals, normed = lax.map(one_block, grouped)]
  transfers between devices with their start and end apart: 6 -> 0, of which waited for: 4 -> 0; matrix products, arithmetic and copies ran while one was open for 9% -> 0% of each run, Pallas kernels for 0% -> 0%
where the time goes in v1:
time: 182 us
  Pallas kernels  172 us (95%)
  local copies, waits for them, and re-layouts  5.08 us (3%)
  other arithmetic  4.83 us (3%)
    pallas_call x1, Pallas kernels, give_back(): pl.pallas_call(give_back_kernel, out_shape=(jax.ShapeDtypeStruct(values.s...  60.9 us
    pallas_call x1, Pallas kernels, spread(): pl.pallas_call(spread_kernel, out_shape=(jax.ShapeDtypeStruct((N_DOC, ROW...  59.1 us
    pallas_call x1, Pallas kernels, attend(): pl.pallas_call(attend_kernel, out_shape=(jax.ShapeDtypeStruct((N_DOC, ROW...  40.5 us
    pallas_call x1, Pallas kernels, merge(): pl.pallas_call(merge_kernel, out_shape=jax.ShapeDtypeStruct((TOK, VW), BF...  11 us

profile of v1, /device:TPU:4, one launch (start us, length us, event | category | flops | bytes accessed | tf_op | source)
XLA Modules:
  0.0 181.6 jit_solution(6642769999684301177)
XLA Ops:
  0.0 0.0 copy-start.2
  0.0 0.0 copy-start.4
  0.0 0.9 select_reduce_fusion
  0.9 0.7 fusion.2
  1.6 0.2 convert_reduce_fusion
  1.8 0.0 copy-start.3
  1.8 0.1 select_reduce_fusion.3
  1.9 0.1 sub.16
  2.0 0.1 add.99
  2.1 0.1 add.100
  2.2 0.1 broadcast_in_dim.115
  2.2 0.1 broadcast_in_dim.127
  2.4 0.1 add.102
  2.5 0.1 broadcast_in_dim.119
  2.5 0.1 broadcast_in_dim.120
  2.6 0.1 broadcast_in_dim.121
  2.7 0.6 pad_add_fusion.tbl_ref
  3.3 1.0 constant_dynamic-update-slice_fusion.1
  4.3 0.9 constant_dynamic-update-slice_fusion.q_ref
  5.2 0.0 copy-start
  5.2 0.8 copy-done
  6.0 59.1 %spread.1 = (bf16[32,32,1536]{2,1,0:T(8,128)(2,1)}, s32[4,8,1,256]{3,2,1,0:T(1,128)}, bf16[16,512,576]{2,1,0:T(8,128)(2,1)}) custom-call(bf16[128,1536]{1,0:T(8,128)(2,1)} %copy-done, s32[8,1,256]{2,1,0:T(1,128)} %pad_add_fusion.tbl_ref, bf16[16,64,576]{2,1,0:T(8,128)(2,1)} %doc_ref.1), custom_call_target="tpu_custom_call" | custom-call | tf_op jit(solution)/shard_map/spread/pallas_call | solution.py:192
  65.1 0.8 reduce
  65.9 0.4 reshape.175
  66.3 0.3 copy.23
  66.6 0.1 fusion
  66.7 0.1 copy.21
  66.8 0.1 reshape.176
  66.9 0.0 copy-done.2
  66.9 0.0 copy-done.4
  66.9 0.2 select_reduce_fusion.1
  67.1 0.7 select_reduce_fusion.4.blk_ref
  67.8 0.5 add_maximum_fusion.code_ref
  68.3 40.5 %attend.1 = (bf16[32,32,1024]{2,1,0:T(8,128)(2,1)}, f32[64,1,128]{2,1,0:T(1,128)}) custom-call(s32[64]{0:T(128)} %add_maximum_fusion.code_ref, s32[64]{0:T(128)} %select_reduce_fusion.4.blk_ref, bf16[32,32,1536]{2,1,0:T(8,128)(2,1)} %get-tuple-element.13.slots_ref, bf16[16,512,576]{2,1,0:T(8,128)(2,1)} %get-tuple-element.14.full_ref, ...), custom_call_target="tpu_custom_call" | custom-call | tf_op jit(solution)/shard_map/attend/pallas_call | solution.py:273
  108.8 0.0 copy-done.3
  108.8 0.0 copy-start.1
  108.8 60.9 %give_back.1 = (bf16[32,32,1024]{2,1,0:T(8,128)(2,1)}, f32[32,2,128]{2,1,0:T(2,128)}) custom-call(bf16[32,32,1024]{2,1,0:T(8,128)(2,1)} %get-tuple-element.15.val_ref, f32[32,2,128]{2,1,0:T(2,128)} %bitcast.9), custom_call_target="tpu_custom_call" | custom-call | tf_op jit(solution)/shard_map/give_back/pallas_call | solution.py:337
  169.7 0.0 copy-done.1
  169.7 0.8 copy.22.ql_ref
  170.5 11.0 %merge.1 = bf16[128,1024]{1,0:T(8,128)(2,1)} custom-call(s32[32]{0:T(128)} %copy-done.3, s32[32]{0:T(128)} %req_ref.1, bf16[128,1536]{1,0:T(8,128)(2,1)} %copy-done, bf16[128,576]{1,0:T(8,128)(2,1)} %copy.22.ql_ref, bf16[8,128,512]{2,1,0:T(8,128)(2,1)} %uk_ref.3, bf16[8,512,128]{2,1,0:T(8,128)(2,1)} %uv_ref.3, bf16[64,16,1024]{2,1,0:T(8,128)(2,1)} %bitcast.8, ...), custom_call_target="tpu_custom_call" | custom-call | tf_op jit(solution)/shard_map/merge/pallas_call | solution.py:400
  (9 shorter events, 0.1 us)
Async XLA Ops:
  0.0 66.9 %copy-start.2 = (s32[512]{0:T(512)S(1)}, s32[512]{0:T(512)}, u32[]{:S(2)}) copy-start(s32[512]{0:T(512)} %param.16) | copy-start | bytes 6148
  0.0 66.9 %copy-start.4 = (s32[512]{0:T(512)S(1)}, s32[512]{0:T(512)}, u32[]{:S(2)}) copy-start(s32[512]{0:T(512)} %param.17) | copy-start | bytes 6148
  1.8 107.0 %copy-start.3 = (s32[32]{0:T(128)}, s32[32]{0:T(128)S(1)}, u32[]{:S(2)}) copy-start(s32[32]{0:T(128)S(1)} %multiply_add_fusion.1.pos_ref) | copy-start | bytes 388
  5.2 0.8 copy-start
  108.8 60.9 %copy-start.1 = (bf16[128,576]{0,1:T(8,128)(2,1)S(1)}, bf16[128,576]{0,1:T(8,128)(2,1)}, u32[]{:S(2)}) copy-start(bf16[128,576]{0,1:T(8,128)(2,1)} %param.12) | copy-start | bytes 442372

commit v2 on v0

v2 whole, which is shorter than its diff:
```python
import jax
import jax.numpy as jnp
from jax import lax
from jax.experimental import pallas as pl
from jax.experimental.pallas import tpu as pltpu
from jax.sharding import PartitionSpec as P

RANK = 512
ROPE = 64
NOPE = 128
VDIM = 128
LATENT = RANK + ROPE
Q_LEN = 16
BLOCK = 128
DOC_LEN = 512
HD = 8
TOK = 128
REQ = 8
DOC_DEV = 16
PAIRS = 32
CAP = 2
ROWS = CAP * Q_LEN
NX, NZ, NY = 4, 8, 4
N_DOC = NX * NZ
SLOTS = N_DOC * CAP
GROUP = NX * CAP
OWN = NZ
NW = HD * NOPE
QW = HD * (NOPE + ROPE)
VW = HD * VDIM
POS = 64
TBL = 3 * NX * ROWS
SCALE = (NOPE + ROPE) ** (-0.5)
LN2 = 0.6931471805599453
EXP2_SCALE = SCALE / LN2
LOWEST = -1e30
MESH = pl.DeviceIdType.MESH
F32 = jnp.float32
BF16 = jnp.bfloat16
VMEM_LIMIT = 58 * 1024 * 1024


def dot(a, b, dims):
    return lax.dot_general(a, b, (dims, ((), ())), preferred_element_type=F32)


def whole_kernel(
    qn_ref, qr_ref, ql_ref, tbl_ref, doc_ref, uk_ref, uv_ref, out_ref,
    full, gq, sendb, slots, tblb, tblx, sm_own, sm_got, qa, qrope, inv, vals, lses,
    xv, xl, pv, plse, inv_v, in_l,
    zs, zr, ts, tr, us, ur, xs, xr, ys, yr, cs, cr, vs, vr, es, er, ps, pr, fs, fr, ls,
):
    d = lax.axis_index("doc")
    h = lax.axis_index("head")
    z, x = d // NX, d % NX
    y, c = h // 2, h % 2
    z_peer = [None] + [(((z + j) % NZ) * NX + x, h) for j in range(1, NZ)]
    x_peer = [None] + [(z * NX + (x + j) % NX, h) for j in range(1, NX)]
    right, left = z_peer[1], z_peer[NZ - 1]
    h_up = ((y + 1) % NY) * 2 + c
    h_down = ((y + NY - 1) % NY) * 2 + c
    h_far = ((y + 2) % NY) * 2 + c
    up, down, other = (d, h_up), (d, h_down), (d, y * 2 + 1 - c)

    barrier = pltpu.get_barrier_semaphore()
    greeted = z_peer[1:] + x_peer[1:] + [up, down, other]
    for peer in greeted:
        pl.semaphore_signal(barrier, inc=1, device_id=peer, device_id_type=MESH)
    gq[0, :, 0:NW] = qn_ref[...]
    gq[0, :, NW:QW] = qr_ref[...]
    tblb[pl.ds(z, 1)] = tbl_ref[pl.ds(z, 1)]
    pl.semaphore_wait(barrier, len(greeted))

    sent = []

    def remote(src, dst, send, recv, peer):
        copy = pltpu.make_async_remote_copy(
            src_ref=src, dst_ref=dst, send_sem=send, recv_sem=recv, device_id=peer, device_id_type=MESH
        )
        copy.start()
        sent.append(copy)
        return copy

    half = TOK // 2
    low, high = pl.ds(0, half), pl.ds(half, half)

    def ring(i, src, dst, peer):
        return remote(src, dst, zs.at[i], zr.at[i], peer)

    ring_a = ring(0, gq.at[0], gq.at[7], right)
    ring_b = ring(1, gq.at[0], gq.at[1], left)
    tables = [
        remote(tbl_ref.at[(z + j) % NZ], tblb.at[z], ts.at[j], tr.at[j], z_peer[j]) for j in range(1, NZ)
    ]

    def place(head):
        return full.at[:, pl.ds(pl.multiple_of(head * POS, POS), POS), :]

    def part(head, first):
        return full.at[pl.ds(first, DOC_DEV // 2), pl.ds(pl.multiple_of(head * POS, POS), POS), :]

    docs_up = remote(doc_ref, place(h), ys.at[0], yr.at[0], up)
    docs_down = remote(doc_ref, place(h), ys.at[1], yr.at[1], down)
    docs_other = remote(doc_ref, place(h), cs.at[0], cr.at[0], other)
    own_docs = pltpu.make_async_copy(doc_ref, place(h), ls.at[0])
    own_docs.start()

    for copy in tables:
        copy.wait_recv()
    passed = [remote(tblb, tblx.at[x], us.at[j], ur.at[j], x_peer[j]) for j in range(1, NX)]
    tblx[pl.ds(x, 1)] = tblb[...].reshape(1, NZ, 1, TBL)
    own_table = pltpu.make_async_copy(tblb, sm_own, ls.at[1])
    own_table.start()

    token = lax.broadcasted_iota(jnp.int32, (TOK, NX * ROWS), 0)
    arriving = {}

    def picked(rel):
        wanted = tblb[(z + rel) % NZ][:, 0:TOK]
        return jnp.where(token == wanted, 1.0, 0.0).astype(BF16)

    def forward(rel):
        pick = picked(rel)
        for k in range(0, QW, 512):
            chosen = dot(pick, gq[rel, :, k : k + 512], ((0,), (0,))).astype(BF16)
            sendb[rel, :, :, k : k + 512] = chosen.reshape(NX, ROWS, 512)
        arriving[rel] = [
            remote(
                sendb.at[rel, (x + j) % NX], slots.at[rel, x], xs.at[rel, j], xr.at[rel, j], x_peer[j]
            )
            for j in range(1, NX)
        ]
        slots[rel, pl.ds(x, 1)] = sendb[rel, pl.ds(x, 1)]

    def absorb(group, rows):
        span = pl.ds(group * GROUP, GROUP)
        for head in range(HD):
            nope = rows(head * NOPE, NOPE).reshape(TOK, NOPE)
            absorbed = dot(nope, uk_ref[head], ((1,), (0,))).astype(BF16)
            qa[span, head] = absorbed.reshape(GROUP, Q_LEN, RANK)
            qrope[span, head] = rows(NW + head * ROPE, ROPE).reshape(GROUP, Q_LEN, ROPE)

    def take_in(rel):
        for copy in arriving[rel]:
            copy.wait_recv()
        absorb(rel, lambda first, width: slots[rel, :, :, first : first + width])

    row = lax.broadcasted_iota(jnp.int32, (TOK, TOK), 0)
    column = lax.broadcasted_iota(jnp.int32, (TOK, TOK), 1)
    diagonal = row == column

    def softmax(scores):
        largest = jnp.max(scores, axis=1, keepdims=True) * EXP2_SCALE
        weights = jnp.exp2(scores * EXP2_SCALE - largest)
        totals = jnp.sum(weights, axis=1, keepdims=True)
        lse = largest * LN2 + jnp.log(totals)
        as_row = jnp.sum(jnp.where(diagonal, lse, 0.0), axis=0, keepdims=True)
        return weights.astype(BF16), 1.0 / totals, as_row

    def finish(slot, i, weights, scale, keys):
        latent = dot(weights, keys, ((1,), (0,)))
        qa[slot] = latent.astype(BF16).reshape(HD, Q_LEN, RANK)
        inv[i] = jnp.broadcast_to(scale, (TOK, VDIM)).reshape(HD, Q_LEN, VDIM)

    def project(group, store):
        for head in range(HD):
            latent = qa[pl.ds(group * GROUP, GROUP), head].reshape(TOK, RANK)
            values = dot(latent, uv_ref[head], ((1,), (0,))) * inv[:, head].reshape(TOK, VDIM)
            store(head * VDIM, values.astype(BF16))

    def own_term():
        absorb(OWN, lambda first, width: gq[0, :, first : first + width])
        key_at = lax.broadcasted_iota(jnp.int32, (TOK, Q_LEN), 1)
        query_at = lax.broadcasted_iota(jnp.int32, (TOK, Q_LEN), 0) % Q_LEN
        for r in range(REQ):
            slot = OWN * GROUP + r
            keys = ql_ref[r * Q_LEN : (r + 1) * Q_LEN, 0:RANK]
            rope_k = ql_ref[r * Q_LEN : (r + 1) * Q_LEN, RANK:LATENT]
            scores = dot(qa[slot].reshape(TOK, RANK), keys, ((1,), (1,))) + dot(
                qrope[slot].reshape(TOK, ROPE), rope_k, ((1,), (1,))
            )
            weights, scale, as_row = softmax(jnp.where(key_at <= query_at, scores, LOWEST))
            lses[OWN, r // CAP, r % CAP : r % CAP + 1] = as_row
            finish(slot, r, weights, scale, keys)

        def store(first, values):
            vals[OWN, :, :, first : first + VDIM] = values.reshape(NX, ROWS, VDIM)

        project(OWN, store)

    key_place = lax.broadcasted_iota(jnp.int32, (1, DOC_LEN), 1)

    def attend(rel):
        owner = (z + rel) % NZ

        def quad(g, carry):
            jobs = []
            for i in range(4):
                source, turn = g * 2 + i // CAP, i % CAP
                first = x * ROWS + turn * Q_LEN
                doc = sm_got[source, owner, 0, TOK + first]
                blocks = sm_got[source, owner, 0, 2 * TOK + first]
                index = g * 4 + i
                slot = rel * GROUP + index
                scores = dot(qa[slot].reshape(TOK, RANK), full[doc, :, 0:RANK], ((1,), (1,))) + dot(
                    qrope[slot].reshape(TOK, ROPE), full[doc, :, RANK:LATENT], ((1,), (1,))
                )
                jobs.append((source, turn, doc, blocks, index, slot, scores))
            soft = []
            for source, turn, doc, blocks, index, slot, scores in jobs:
                hide = jnp.where(key_place < blocks * BLOCK, 0.0, LOWEST)
                soft.append(softmax(scores + hide))
            for (source, turn, doc, blocks, index, slot, scores), (weights, scale, as_row) in zip(jobs, soft):
                lses[rel, source, turn : turn + 1] = as_row
                finish(slot, index, weights, scale, full[doc, :, 0:RANK])
            return carry

        lax.fori_loop(0, GROUP // 4, quad, 0)

        def store(first, values):
            vals[rel, :, :, first : first + VDIM] = values.reshape(NX, ROWS, VDIM)

        project(rel, store)

    returning = {}

    def hand_over(rel):
        returning[rel] = []
        for j in range(1, NX):
            peer = (x + j) % NX
            returning[rel] += [
                remote(vals.at[rel, peer], xv.at[rel, x], vs.at[rel, j], vr.at[rel, j], x_peer[j]),
                remote(lses.at[rel, peer], xl.at[rel, x], es.at[rel, j], er.at[rel, j], x_peer[j]),
            ]
        xv[rel, pl.ds(x, 1)] = vals[rel, pl.ds(x, 1)]
        xl[rel, pl.ds(x, 1)] = lses[rel, pl.ds(x, 1)]

    request_at = lax.broadcasted_iota(jnp.int32, (REQ, TOK), 0) * Q_LEN

    def merge(rel, partials, store):
        for copy in returning[rel]:
            copy.wait_recv()
        owner = (z + rel) % NZ
        pick = picked(rel)
        hits, rows = [], []
        for s in range(GROUP):
            hits.append(request_at == sm_own[owner, 0, s * Q_LEN])
            rows.append(xl[rel, s // CAP, s % CAP : s % CAP + 1])
        top = jnp.full((REQ, TOK), LOWEST, F32)
        for _, lse in partials:
            top = jnp.maximum(top, lse)
        for hit, lse in zip(hits, rows):
            top = jnp.maximum(top, jnp.where(hit, lse, LOWEST))
        part_share = [jnp.exp(lse - top) for _, lse in partials]
        slot_share = [jnp.where(hit, jnp.exp(lse - top), 0.0) for hit, lse in zip(hits, rows)]
        total = jnp.maximum(sum(part_share + slot_share), 1e-30)
        scale = 1.0 / total
        shares = [share * scale for share in part_share] + [
            jnp.sum(share * scale, axis=0, keepdims=True) for share in slot_share
        ]
        turned = jnp.transpose(jnp.concatenate(shares, axis=0))
        count = len(partials)
        for head in range(HD):
            mine = turned[head * Q_LEN : (head + 1) * Q_LEN]

            def stacked(first):
                return jnp.concatenate([mine[:, k : k + 1] for k in range(first, first + REQ)], axis=0)

            at = head * VDIM
            slot_values = xv[rel, :, :, at : at + VDIM].reshape(TOK, VDIM).astype(F32)
            scaled = (slot_values * stacked(count * REQ)).astype(BF16)
            result = dot(pick, scaled, ((1,), (0,)))
            for k, (values, _) in enumerate(partials):
                result = result + values(at).astype(F32) * stacked(k * REQ)
            store(at, result.astype(BF16))
        return top + jnp.log(total)

    def incoming(i):
        return (lambda at: inv_v[i, :, at : at + VDIM]), in_l[i].reshape(REQ, TOK)

    falling = {}

    def pass_on(rel, span, span_l, target, i, peer):
        falling[i] = [
            remote(pv.at[rel, span], inv_v.at[target, span], ps.at[i], pr.at[i], peer),
            remote(plse.at[rel, span_l], in_l.at[target, span_l], fs.at[i], fr.at[i], peer),
        ]

    def settle(rel, awaited):
        partials = []
        if awaited is not None:
            for copy in falling[awaited]:
                copy.wait_recv()
            partials = [incoming(rel)]

        def store(at, values):
            pv[rel, :, at : at + VDIM] = values

        plse[rel] = merge(rel, partials, store).reshape(2, REQ // 2, TOK)

    everything, both = pl.ds(0, TOK), pl.ds(0, 2)
    inv_v[3, half:TOK] = jnp.zeros((half, VW), BF16)
    inv_v[5, 0:half] = jnp.zeros((half, VW), BF16)
    in_l[3, 1] = jnp.full((REQ // 2, TOK), LOWEST, F32)
    in_l[5, 0] = jnp.full((REQ // 2, TOK), LOWEST, F32)

    forward(0)
    own_term()
    ring_a.wait_recv()
    ring_a = ring(2, gq.at[7], gq.at[6], right)
    ring_b.wait_recv()
    ring_b = ring(3, gq.at[1], gq.at[2], left)
    forward(7)
    forward(1)
    take_in(0)
    for copy in passed:
        copy.wait_recv()
    got_table = pltpu.make_async_copy(tblx, sm_got, ls.at[2])
    got_table.start()
    ring_a.wait_recv()
    ring_a = ring(4, gq.at[6], gq.at[5], right)
    ring_b.wait_recv()
    ring_b = ring(5, gq.at[2], gq.at[3], left)
    forward(6)
    forward(2)
    take_in(7)
    take_in(1)
    ring_a.wait_recv()
    ring_a = ring(6, gq.at[5, low], gq.at[4, low], right)
    ring_b.wait_recv()
    ring_b = ring(7, gq.at[3, high], gq.at[4, high], left)
    forward(5)
    forward(3)
    take_in(6)
    take_in(2)

    docs_up.wait_recv()
    pass_up = remote(part(h_down, 0), part(h_down, 0), ys.at[2], yr.at[2], up)
    cross_down = remote(place(h_down), place(h_down), cs.at[1], cr.at[1], other)
    docs_down.wait_recv()
    pass_down = remote(part(h_up, 8), part(h_up, 8), ys.at[3], yr.at[3], down)
    cross_up = remote(place(h_up), place(h_up), cs.at[2], cr.at[2], other)

    ring_a.wait_recv()
    ring_b.wait_recv()
    forward(4)
    take_in(5)
    take_in(3)

    pass_up.wait_recv()
    pass_down.wait_recv()
    cross_far = remote(place(h_far), place(h_far), cs.at[3], cr.at[3], other)
    take_in(4)
    own_docs.wait()
    own_table.wait()
    got_table.wait()
    for copy in (docs_other, cross_down, cross_up, cross_far):
        copy.wait_recv()

    attend(4)
    hand_over(4)
    attend(3)
    hand_over(3)
    settle(4, None)
    pass_on(4, low, pl.ds(0, 1), 3, 0, right)
    pass_on(4, high, pl.ds(1, 1), 5, 1, left)
    attend(5)
    hand_over(5)
    settle(3, 0)
    pass_on(3, everything, both, 2, 2, right)
    attend(2)
    hand_over(2)
    settle(5, 1)
    pass_on(5, everything, both, 6, 3, left)
    attend(6)
    hand_over(6)
    settle(2, 2)
    pass_on(2, everything, both, 1, 4, right)
    attend(1)
    hand_over(1)
    settle(6, 3)
    pass_on(6, everything, both, 7, 5, left)
    attend(7)
    hand_over(7)
    settle(1, 4)
    pass_on(1, everything, both, 0, 6, right)
    attend(0)
    hand_over(0)
    settle(7, 5)
    pass_on(7, everything, both, 4, 7, left)
    for copy in falling[6] + falling[7]:
        copy.wait_recv()

    def own_values(at):
        return vals[OWN, :, :, at : at + VDIM].reshape(TOK, VDIM)

    def store(at, values):
        out_ref[:, at : at + VDIM] = values

    merge(0, [incoming(0), incoming(4), (own_values, lses[OWN].reshape(REQ, TOK))], store)
    for copy in sent:
        copy.wait_send()


def whole(q_nope, q_rope, question_latent, table, doc_cache, w_uk, w_uv):
    local = pl.BlockSpec(memory_space=pltpu.VMEM)
    anywhere = pl.BlockSpec(memory_space=pl.ANY)
    dma = pltpu.SemaphoreType.DMA
    return pl.pallas_call(
        whole_kernel,
        out_shape=jax.ShapeDtypeStruct((TOK, VW), BF16),
        in_specs=[local, local, local, local, anywhere, local, local],
        out_specs=local,
        scratch_shapes=[
            pltpu.VMEM((DOC_DEV, DOC_LEN, LATENT), BF16),
            pltpu.VMEM((NZ, TOK, QW), BF16),
            pltpu.VMEM((NZ, NX, ROWS, QW), BF16),
            pltpu.VMEM((NZ, NX, ROWS, QW), BF16),
            pltpu.VMEM((NZ, 1, TBL), jnp.int32),
            pltpu.VMEM((NX, NZ, 1, TBL), jnp.int32),
            pltpu.SMEM((NZ, 1, TBL), jnp.int32),
            pltpu.SMEM((NX, NZ, 1, TBL), jnp.int32),
            pltpu.VMEM(((NZ + 1) * GROUP, HD, Q_LEN, RANK), BF16),
            pltpu.VMEM(((NZ + 1) * GROUP, HD, Q_LEN, ROPE), BF16),
            pltpu.VMEM((GROUP, HD, Q_LEN, VDIM), F32),
            pltpu.VMEM((NZ + 1, NX, ROWS, VW), BF16),
            pltpu.VMEM((NZ + 1, NX, CAP, TOK), F32),
            pltpu.VMEM((NZ, NX, ROWS, VW), BF16),
            pltpu.VMEM((NZ, NX, CAP, TOK), F32),
            pltpu.VMEM((NZ, TOK, VW), BF16),
            pltpu.VMEM((NZ, 2, REQ // 2, TOK), F32),
            pltpu.VMEM((NZ, TOK, VW), BF16),
            pltpu.VMEM((NZ, 2, REQ // 2, TOK), F32),
            dma((8,)), dma((8,)),
            dma((NZ,)), dma((NZ,)),
            dma((NX,)), dma((NX,)),
            dma((NZ, NX)), dma((NZ, NX)),
            dma((4,)), dma((4,)),
            dma((4,)), dma((4,)),
            dma((NZ, NX)), dma((NZ, NX)),
            dma((NZ, NX)), dma((NZ, NX)),
            dma((8,)), dma((8,)),
            dma((8,)), dma((8,)),
            dma((3,)),
        ],
        compiler_params=pltpu.CompilerParams(
            collective_id=0, has_side_effects=True, vmem_limit_bytes=VMEM_LIMIT
        ),
        name="whole",
    )(q_nope, q_rope, question_latent, table, doc_cache, w_uk, w_uv)


def on_device(
    q_nope, q_rope, question_latent, doc_cache, w_uk, w_uv, doc_slot, doc_blocks, pair_doc, pair_req
):
    doc_ids = jnp.arange(doc_slot.shape[0], dtype=jnp.int32)
    matches = pair_doc[:, None] == doc_ids[None, :]
    pair_slot = jnp.sum(jnp.where(matches, doc_slot[None, :], 0), axis=1)
    pair_blocks = jnp.sum(jnp.where(matches, doc_blocks[None, :], 0), axis=1)
    target = pair_slot // DOC_DEV
    sequence = jnp.arange(PAIRS, dtype=jnp.int32)
    before = (target[:, None] == target[None, :]) & (sequence[None, :] < sequence[:, None])
    position = target * CAP + jnp.sum(before.astype(jnp.int32), axis=1)
    placed = jnp.arange(SLOTS, dtype=jnp.int32)[:, None] == position[None, :]

    def per_slot(values):
        return jnp.sum(jnp.where(placed, values[None, :], 0), axis=1)[:, None]

    first_token = per_slot(pair_req * Q_LEN + 1) - 1
    places = jnp.arange(Q_LEN, dtype=jnp.int32)
    tokens = jnp.where(first_token >= 0, first_token + places, -1)
    doc = jnp.broadcast_to(per_slot(pair_slot % DOC_DEV), (SLOTS, Q_LEN))
    blocks = jnp.broadcast_to(per_slot(pair_blocks), (SLOTS, Q_LEN))
    table = jnp.concatenate(
        [part.reshape(NZ, 1, NX * ROWS) for part in (tokens, doc, blocks)], axis=2
    )
    return whole(q_nope, q_rope, question_latent, table, doc_cache, w_uk, w_uv)


def solution(mesh):
    placed = (
        P("doc", "head"),
        P("doc", "head"),
        P("doc", None),
        P("doc", "head", None),
        P("head", None, None),
        P("head", None, None),
        P(),
        P(),
        P("doc"),
        P("doc"),
    )
    return jax.shard_map(
        on_device, mesh=mesh, in_specs=placed, out_specs=P("doc", "head"), check_vma=False
    )
```

time: 556 us -> 119 us (0.21)
  waiting for transfers between devices: 259 us -> 0 us
  Pallas kernels: 0 us -> 111 us
  local copies, waits for them, and re-layouts: 111 us -> 4.37 us
  matrix products: 71.4 us -> 0 us
  starting transfers between devices: 53.2 us -> 0 us
  other arithmetic: 45.2 us -> 2.49 us
  between operations: 13.8 us -> 0.04 us
    all_to_all x5 -> x0, waiting for transfers between devices: 258 us -> none  [the longest x1 206 us: on_device(): lax.all_to_all(outgoing.reshape(peer_count, capacity, Q_LEN, head_count *...]
    pallas_call x0 -> x1, Pallas kernels: none -> 111 us  [whole(): pl.pallas_call(whole_kernel, out_shape=jax.ShapeDtypeStruct((TOK, VW), BF...]
    dot_general x20 -> x0, matrix products: 71.4 us -> none  [the longest x9 34.2 us: attend(): jnp.einsum('bqhc,blc->bqhl', queries, key_rows, preferred_element_type=jn...]
    gather x9 -> x0, local copies, waits for them, and re-layouts: 66 us -> none  [the longest x8 60 us: one_block(): key_rows = jnp.take(table, block_picked, axis=0)]
    all_to_all x5 -> x0, starting transfers between devices: 53.1 us -> none  [the longest x1 19.3 us: on_device(): lax.all_to_all(maxima.reshape(peer_count, capacity, answer_item_count, he...]
    select_n x19 -> x2, other arithmetic: 33.1 us -> 0.69 us  [the longest x1 0.67 us: on_device(): doc = jnp.broadcast_to(per_slot(pair_slot % DOC_DEV), (SLOTS, Q_LEN))]
    another operation x2 -> x0, local copies, waits for them, and re-layouts: 21.9 us -> none  [the longest x1 17.7 us: slot_partials(): queries.reshape((blocks, slot_group) + queries.shape[1:])]
    dynamic_update_slice x32 -> x0, local copies, waits for them, and re-layouts: 8.37 us -> none  [slot_partials(): maxima, totals, normed = lax.map(one_block, grouped)]
  transfers between devices with their start and end apart: 6 -> 0, of which waited for: 4 -> 0; matrix products, arithmetic and copies ran while one was open for 9% -> 0% of each run, Pallas kernels for 0% -> 0%
where the time goes in v2:
time: 119 us; the launch traced here: 117 us
  Pallas kernels  111 us (93%)
  local copies, waits for them, and re-layouts  4.37 us (4%)
  other arithmetic  2.49 us (2%)
    pallas_call x1, Pallas kernels, whole(): pl.pallas_call(whole_kernel, out_shape=jax.ShapeDtypeStruct((TOK, VW), BF...  111 us
    unnamed x2, local copies, waits for them, and re-layouts  3.38 us

profile of v2, /device:TPU:4, one launch (start us, length us, event | category | flops | bytes accessed | tf_op | source)
XLA Modules:
  0.0 117.4 jit_solution(11804546156420719313)
XLA Ops:
  0.0 0.9 select_reduce_fusion.1
  0.9 0.7 and_select_fusion
  1.6 0.2 convert_reduce_fusion
  1.8 0.1 select_reduce_fusion.4
  1.9 0.1 sub.14
  2.0 0.1 broadcast_in_dim.104
  2.0 0.1 broadcast_in_dim.99
  2.1 0.1 add.74
  2.2 0.1 broadcast_in_dim.95
  2.3 0.1 broadcast_in_dim.107
  2.4 0.1 broadcast_in_dim.100
  2.5 0.1 broadcast_in_dim.101
  2.6 0.1 broadcast_in_dim.105
  2.6 0.1 broadcast_in_dim.106
  2.7 0.1 add.71
  2.8 0.1 add.72
  2.9 0.6 pad_add_fusion.tbl_ref
  3.5 1.7 %copy.15.ql_ref = bf16[128,576]{1,0:T(8,128)(2,1)} copy(bf16[128,576]{0,1:T(8,128)(2,1)} %param.12) | data formatting | bytes 294912 | tf_op args[2]
  5.2 110.5 %whole.1 = bf16[128,1024]{1,0:T(8,128)(2,1)} custom-call(bf16[128,1024]{1,0:T(8,128)(2,1)} %qn_ref.1, bf16[128,512]{1,0:T(8,128)(2,1)} %qr_ref.1, bf16[128,576]{1,0:T(8,128)(2,1)} %copy.15.ql_ref, s32[8,1,384]{2,1,0:T(1,128)} %pad_add_fusion.tbl_ref, bf16[16,64,576]{2,1,0:T(8,128)(2,1)} %doc_ref.1, bf16[8,128,512]{2,1,0:T(8,128)(2,1)} %uk_ref.1, ...), custom_call_target="tpu_custom_call" | custom-call | tf_op jit(solution)/shard_map/whole/pallas_call | solution.py:409
  115.8 1.7 %copy.17 = bf16[128,1024]{1,0:T(8,128)(2,1)} copy(bf16[128,1024]{1,0:T(8,128)(2,1)} %whole.1) | data formatting | bytes 524288
  (5 shorter events, 0.0 us)

commit v3 on v2

v3 whole, which is shorter than its diff:
```python
import jax
import jax.numpy as jnp
from jax import lax
from jax.experimental import pallas as pl
from jax.experimental.pallas import tpu as pltpu
from jax.sharding import PartitionSpec as P

RANK = 512
ROPE = 64
NOPE = 128
VDIM = 128
LATENT = RANK + ROPE
Q_LEN = 16
BLOCK = 128
DOC_LEN = 512
HD = 8
TOK = 128
REQ = 8
DOC_DEV = 16
PAIRS = 32
CAP = 2
ROWS = CAP * Q_LEN
NX, NZ, NY = 4, 8, 4
N_DOC = NX * NZ
SLOTS = N_DOC * CAP
GROUP = NX * CAP
CHUNKS = 4
HALVES = 2
OWN = NZ
NW = HD * NOPE
QW = HD * (NOPE + ROPE)
VW = HD * VDIM
POS = 64
LANES = 128
TBL = 3 * NX * ROWS
SCALE = (NOPE + ROPE) ** (-0.5)
LN2 = 0.6931471805599453
EXP2_SCALE = SCALE / LN2
LOWEST = -1e30
MESH = pl.DeviceIdType.MESH
F32 = jnp.float32
BF16 = jnp.bfloat16
VMEM_LIMIT = 58 * 1024 * 1024


def dot(a, b, dims):
    return lax.dot_general(a, b, (dims, ((), ())), preferred_element_type=F32)


def whole_kernel(
    qn_ref, qr_ref, qlt_ref, doc_ref, uk_hbm, uv_hbm, slot_ref, blocks_ref, name_ref, request_ref, out_ref,
    full_lat, full_rope, doc_in, uk_ref, uv_ref, ql, gq, sendb, slots, tbl, tblb, tblx, sm_own, sm_got,
    qa, q_lo, q_hi, inv, vals, lses, xv, xl, pv, plse, in_v, in_l,
    zs, zr, ts, tr, us, ur, xs, xr, ys, yr, cs, cr, vs, vr, es, er, ps, pr, fs, fr, ls,
):
    d = lax.axis_index("doc")
    h = lax.axis_index("head")
    z, x = d // NX, d % NX
    y, c = h // 2, h % 2
    z_peer = [None] + [(((z + j) % NZ) * NX + x, h) for j in range(1, NZ)]
    x_peer = [None] + [(z * NX + (x + j) % NX, h) for j in range(1, NX)]
    right, left = z_peer[1], z_peer[NZ - 1]
    h_up = ((y + 1) % NY) * 2 + c
    h_down = ((y + NY - 1) % NY) * 2 + c
    h_far = ((y + 2) % NY) * 2 + c
    up, down, other = (d, h_up), (d, h_down), (d, y * 2 + 1 - c)

    barrier = pltpu.get_barrier_semaphore()
    greeted = z_peer[1:] + x_peer[1:] + [up, down, other]
    for peer in greeted:
        pl.semaphore_signal(barrier, inc=1, device_id=peer, device_id_type=MESH)

    def here(src, dst, i):
        copy = pltpu.make_async_copy(src, dst, ls.at[i])
        copy.start()
        return copy

    doc_lat = doc_ref.at[:, :, :, pl.ds(0, RANK)]

    def lat(head, first=0, count=DOC_DEV):
        return full_lat.at[pl.ds(first, count), :, head]

    def rope(head, first=0, count=DOC_DEV):
        return full_rope.at[pl.ds(first, count), head]

    queries_in = [
        here(qn_ref, gq.at[0, :, pl.ds(0, NW)], 0),
        here(qr_ref, gq.at[0, :, pl.ds(NW, QW - NW)], 1),
    ]
    docs_in = here(doc_ref, doc_in, 2)
    own_lat = here(doc_lat, lat(h), 3)
    weights_in = [here(uk_hbm, uk_ref, 4), here(uv_hbm, uv_ref, 5)]
    for copy in queries_in:
        copy.wait()
    pl.semaphore_wait(barrier, len(greeted))

    sent = []

    def remote(src, dst, send, recv, peer):
        copy = pltpu.make_async_remote_copy(
            src_ref=src, dst_ref=dst, send_sem=send, recv_sem=recv, device_id=peer, device_id_type=MESH
        )
        copy.start()
        sent.append(copy)
        return copy

    half = TOK // 2
    low, high = pl.ds(0, half), pl.ds(half, half)
    chain = ((0, 7, 6, 5, 4), (0, 1, 2, 3, 4))
    hops = {}

    def hop(way, step, k):
        rows = pl.ds(k * (TOK // CHUNKS), TOK // CHUNKS)
        hops[way, step, k] = remote(
            gq.at[chain[way][step], rows], gq.at[chain[way][step + 1], rows],
            zs.at[way, step, k], zr.at[way, step, k], (right, left)[way],
        )

    for k in range(CHUNKS):
        hop(0, 0, k)
        hop(1, 0, k)

    def advance(step):
        for k in range(CHUNKS):
            for way in range(2):
                hops[way, step - 1, k].wait_recv()
                if step < 3 or (k < CHUNKS // 2) == (way == 0):
                    hop(way, step, k)

    part = DOC_DEV // CHUNKS
    docs_up, docs_down, pass_up, pass_down, crossed = {}, {}, {}, {}, []

    def cross(src):
        i = len(crossed)
        crossed.append(remote(src, src, cs.at[i], cr.at[i], other))

    def doc_part(k):
        return doc_ref.at[pl.ds(k * part, part), :, :, pl.ds(0, RANK)]

    for e in range(CHUNKS):
        k, m = e, (e + 2) % CHUNKS
        docs_up[k] = remote(doc_part(k), lat(h, k * part, part), ys.at[0, k], yr.at[0, k], up)
        docs_down[m] = remote(doc_part(m), lat(h, m * part, part), ys.at[1, m], yr.at[1, m], down)
    crossed.append(remote(doc_lat, lat(h), cs.at[0], cr.at[0], other))

    lane = lax.broadcasted_iota(jnp.int32, (NZ, TOK), 1)
    channel = lax.broadcasted_iota(jnp.int32, (NZ, TOK), 0) * NX + lane // ROWS
    turn_at = (lane % ROWS) // Q_LEN
    token_at = lane % Q_LEN

    def route(k, carry):
        tokens, docs, blocks, filled = carry
        name = name_ref[k]
        place = slot_ref[name]
        mine = channel == place // DOC_DEV
        put = mine & (turn_at == filled)
        return (
            jnp.where(put, request_ref[k] * Q_LEN + token_at, tokens),
            jnp.where(put, place % DOC_DEV, docs),
            jnp.where(put, blocks_ref[name], blocks),
            jnp.where(mine, filled + 1, filled),
        )

    nothing = jnp.zeros((NZ, TOK), jnp.int32)
    routed = lax.fori_loop(0, PAIRS, route, (nothing - 1, nothing, nothing, nothing))
    for k in range(3):
        tbl[:, :, k * TOK : (k + 1) * TOK] = routed[k].reshape(NZ, 1, TOK)
    tables = [
        remote(tbl.at[(z + j) % NZ], tblb.at[z], ts.at[j], tr.at[j], z_peer[j]) for j in range(1, NZ)
    ]
    tblb[pl.ds(z, 1)] = tbl[pl.ds(z, 1)]

    docs_in.wait()
    packed = jnp.concatenate([doc_in[:, 0, :, RANK:LATENT], doc_in[:, 1, :, RANK:LATENT]], axis=2)
    full_rope[:, pl.ds(h, 1)] = packed.reshape(DOC_DEV, 1, POS // 2, LANES)
    rope_up = remote(rope(h), rope(h), ys.at[0, 4], yr.at[0, 4], up)
    rope_down = remote(rope(h), rope(h), ys.at[1, 4], yr.at[1, 4], down)
    cross(rope(h))

    for copy in tables:
        copy.wait_recv()
    passed = [remote(tblb, tblx.at[x], us.at[j], ur.at[j], x_peer[j]) for j in range(1, NX)]
    tblx[pl.ds(x, 1)] = tblb[...].reshape(1, NZ, 1, TBL)
    own_table = here(tblb, sm_own, 6)

    token = lax.broadcasted_iota(jnp.int32, (TOK, NX * ROWS), 0)
    arriving = {}

    def picked(rel):
        wanted = tblb[(z + rel) % NZ][:, 0:TOK]
        return jnp.where(token == wanted, 1.0, 0.0).astype(BF16)

    def forward(rel):
        pick = picked(rel)
        for k in range(0, QW, 512):
            chosen = dot(pick, gq[rel, :, k : k + 512], ((0,), (0,))).astype(BF16)
            sendb[rel, :, :, k : k + 512] = chosen.reshape(NX, ROWS, 512)
        arriving[rel] = [
            remote(
                sendb.at[rel, (x + j) % NX], slots.at[rel, x], xs.at[rel, j], xr.at[rel, j], x_peer[j]
            )
            for j in range(1, NX)
        ]
        slots[rel, pl.ds(x, 1)] = sendb[rel, pl.ds(x, 1)]

    def absorb(group, rows):
        span = pl.ds(group * GROUP, GROUP)
        blank = jnp.zeros((TOK, ROPE), BF16)
        for head in range(HD):
            nope = rows(head * NOPE, NOPE).reshape(TOK, NOPE)
            absorbed = dot(nope, uk_ref[head], ((1,), (0,))).astype(BF16)
            qa[span, head] = absorbed.reshape(GROUP, Q_LEN, RANK)
            turned = rows(NW + head * ROPE, ROPE).reshape(TOK, ROPE)
            q_lo[span, head] = jnp.concatenate([turned, blank], axis=1).reshape(GROUP, Q_LEN, LANES)
            q_hi[span, head] = jnp.concatenate([blank, turned], axis=1).reshape(GROUP, Q_LEN, LANES)

    def take_in(rel):
        for copy in arriving[rel]:
            copy.wait_recv()
        absorb(rel, lambda first, width: slots[rel, :, :, first : first + width])

    row = lax.broadcasted_iota(jnp.int32, (TOK, TOK), 0)
    column = lax.broadcasted_iota(jnp.int32, (TOK, TOK), 1)
    diagonal = row == column

    def softmax(scores):
        largest = jnp.max(scores, axis=1, keepdims=True) * EXP2_SCALE
        weights = jnp.exp2(scores * EXP2_SCALE - largest)
        totals = jnp.sum(weights, axis=1, keepdims=True)
        lse = largest * LN2 + jnp.log(totals)
        as_row = jnp.sum(jnp.where(diagonal, lse, 0.0), axis=0, keepdims=True)
        return weights.astype(BF16), 1.0 / totals, as_row

    def finish(slot, i, weights, scale, keys):
        latent = dot(weights, keys, ((1,), (0,)))
        qa[slot] = latent.astype(BF16).reshape(HD, Q_LEN, RANK)
        inv[i] = jnp.broadcast_to(scale, (TOK, VDIM)).reshape(HD, Q_LEN, VDIM)

    def project(group, part_of):
        for j in range(HD // HALVES):
            head = part_of * (HD // HALVES) + j
            latent = qa[pl.ds(group * GROUP, GROUP), head].reshape(TOK, RANK)
            values = dot(latent, uv_ref[head], ((1,), (0,))) * inv[:, head].reshape(TOK, VDIM)
            vals[group, part_of, :, :, j * VDIM : (j + 1) * VDIM] = values.astype(BF16).reshape(
                NX, ROWS, VDIM
            )

    def own_term():
        for k in range(0, LATENT, LANES):
            width = min(LANES, LATENT - k)
            ql[:, k : k + width] = jnp.transpose(qlt_ref[k : k + width].astype(F32)).astype(BF16)
        absorb(OWN, lambda first, width: gq[0, :, first : first + width])
        key_at = lax.broadcasted_iota(jnp.int32, (TOK, Q_LEN), 1)
        query_at = lax.broadcasted_iota(jnp.int32, (TOK, Q_LEN), 0) % Q_LEN
        for r in range(REQ):
            slot = OWN * GROUP + r
            keys = ql[r * Q_LEN : (r + 1) * Q_LEN, 0:RANK]
            rope_k = ql[r * Q_LEN : (r + 1) * Q_LEN, RANK:LATENT]
            turned = q_lo[slot].reshape(TOK, LANES)[:, 0:ROPE]
            scores = dot(qa[slot].reshape(TOK, RANK), keys, ((1,), (1,))) + dot(
                turned, rope_k, ((1,), (1,))
            )
            weights, scale, as_row = softmax(jnp.where(key_at <= query_at, scores, LOWEST))
            lses[OWN, r // CAP, r % CAP : r % CAP + 1] = as_row
            finish(slot, r, weights, scale, keys)
        for p in range(HALVES):
            project(OWN, p)

    key_block = lax.broadcasted_iota(jnp.int32, (1, DOC_LEN), 1) % (DOC_LEN // 2) // (BLOCK // 2)
    returning = {}

    def attend(rel):
        owner = (z + rel) % NZ

        def quad(g, carry):
            jobs = []
            for i in range(4):
                source, turn = g * 2 + i // CAP, i % CAP
                first = x * ROWS + turn * Q_LEN
                doc = sm_got[source, owner, 0, TOK + first]
                blocks = sm_got[source, owner, 0, 2 * TOK + first]
                index = g * 4 + i
                slot = rel * GROUP + index
                keys = full_lat[doc].reshape(DOC_LEN, RANK)
                turned = full_rope[doc].reshape(DOC_LEN // 2, LANES)
                scores = dot(qa[slot].reshape(TOK, RANK), keys, ((1,), (1,))) + jnp.concatenate(
                    [
                        dot(q_lo[slot].reshape(TOK, LANES), turned, ((1,), (1,))),
                        dot(q_hi[slot].reshape(TOK, LANES), turned, ((1,), (1,))),
                    ],
                    axis=1,
                )
                jobs.append((source, turn, doc, blocks, index, slot, scores))
            soft = []
            for source, turn, doc, blocks, index, slot, scores in jobs:
                hide = jnp.where(key_block < blocks, 0.0, LOWEST)
                soft.append(softmax(scores + hide))
            for (source, turn, doc, blocks, index, slot, scores), (weights, scale, as_row) in zip(jobs, soft):
                lses[rel, source, turn : turn + 1] = as_row
                finish(slot, index, weights, scale, full_lat[doc].reshape(DOC_LEN, RANK))
            return carry

        lax.fori_loop(0, GROUP // 4, quad, 0)
        returning[rel] = [
            [
                remote(lses.at[rel, (x + j) % NX], xl.at[rel, x], es.at[rel, j], er.at[rel, j], x_peer[j])
                for j in range(1, NX)
            ]
        ]
        xl[rel, pl.ds(x, 1)] = lses[rel, pl.ds(x, 1)]
        for p in range(HALVES):
            project(rel, p)
            returning[rel].append(
                [
                    remote(
                        vals.at[rel, p, (x + j) % NX], xv.at[rel, p, x],
                        vs.at[rel, p, j], vr.at[rel, p, j], x_peer[j],
                    )
                    for j in range(1, NX)
                ]
            )
            xv[rel, p, pl.ds(x, 1)] = vals[rel, p, pl.ds(x, 1)]

    request_at = lax.broadcasted_iota(jnp.int32, (REQ, TOK), 0) * Q_LEN

    def merge(rel, partials, lse_done, half_ready, store, half_done):
        owner = (z + rel) % NZ
        pick = picked(rel)
        for copy in returning[rel][0]:
            copy.wait_recv()
        hits, rows = [], []
        for s in range(GROUP):
            hits.append(request_at == sm_own[owner, 0, s * Q_LEN])
            rows.append(xl[rel, s // CAP, s % CAP : s % CAP + 1])
        top = jnp.full((REQ, TOK), LOWEST, F32)
        for _, lse in partials:
            top = jnp.maximum(top, lse)
        for hit, lse in zip(hits, rows):
            top = jnp.maximum(top, jnp.where(hit, lse, LOWEST))
        part_share = [jnp.exp(lse - top) for _, lse in partials]
        slot_share = [jnp.where(hit, jnp.exp(lse - top), 0.0) for hit, lse in zip(hits, rows)]
        total = jnp.maximum(sum(part_share + slot_share), 1e-30)
        lse_done(top + jnp.log(total))
        scale = 1.0 / total
        shares = [share * scale for share in part_share] + [
            jnp.sum(share * scale, axis=0, keepdims=True) for share in slot_share
        ]
        turned = jnp.transpose(jnp.concatenate(shares, axis=0))
        count = len(partials)
        for p in range(HALVES):
            for copy in returning[rel][1 + p]:
                copy.wait_recv()
            half_ready(p)
            for j in range(HD // HALVES):
                head = p * (HD // HALVES) + j
                mine = turned[head * Q_LEN : (head + 1) * Q_LEN]

                def stacked(first):
                    return jnp.concatenate([mine[:, k : k + 1] for k in range(first, first + REQ)], axis=0)

                at = j * VDIM
                slot_values = xv[rel, p, :, :, at : at + VDIM].reshape(TOK, VDIM).astype(F32)
                scaled = (slot_values * stacked(count * REQ)).astype(BF16)
                result = dot(pick, scaled, ((1,), (0,)))
                for k, (values, _) in enumerate(partials):
                    result = result + values(p, at).astype(F32) * stacked(k * REQ)
                store(p, at, result.astype(BF16))
            half_done(p)

    def incoming(i):
        return (lambda p, at: in_v[i, p, :, at : at + VDIM]), in_l[i].reshape(REQ, TOK)

    falling_l, falling_v = {}, {}
    everything, both = pl.ds(0, TOK), pl.ds(0, 2)

    def settle(rel, awaited, moves):
        def lse_done(lse):
            plse[rel] = lse.reshape(2, REQ // 2, TOK)
            for i, target, span, span_l, peer in moves:
                falling_l[i] = remote(
                    plse.at[rel, span_l], in_l.at[target, span_l], fs.at[i], fr.at[i], peer
                )

        def half_ready(p):
            if awaited is not None:
                falling_v[awaited, p].wait_recv()

        def store(p, at, values):
            pv[rel, p, :, at : at + VDIM] = values

        def half_done(p):
            for i, target, span, span_l, peer in moves:
                falling_v[i, p] = remote(
                    pv.at[rel, p, span], in_v.at[target, p, span], ps.at[i, p], pr.at[i, p], peer
                )

        partials = []
        if awaited is not None:
            falling_l[awaited].wait_recv()
            partials = [incoming(rel)]
        merge(rel, partials, lse_done, half_ready, store, half_done)

    in_v[3, :, half:TOK] = jnp.zeros((HALVES, half, VW // HALVES), BF16)
    in_v[5, :, 0:half] = jnp.zeros((HALVES, half, VW // HALVES), BF16)
    in_l[3, 1] = jnp.full((REQ // 2, TOK), LOWEST, F32)
    in_l[5, 0] = jnp.full((REQ // 2, TOK), LOWEST, F32)

    def docs_event(e):
        k, m = e, (e + 2) % CHUNKS
        docs_up[k].wait_recv()
        if e < CHUNKS // 2:
            span = lat(h_down, k * part, part)
            pass_up[e] = remote(span, span, ys.at[0, 5 + e], yr.at[0, 5 + e], up)
        cross(lat(h_down, k * part, part))
        docs_down[m].wait_recv()
        if e < CHUNKS // 2:
            span = lat(h_up, m * part, part)
            pass_down[e] = remote(span, span, ys.at[1, 5 + e], yr.at[1, 5 + e], down)
        cross(lat(h_up, m * part, part))

    forward(0)
    for copy in weights_in:
        copy.wait()
    own_term()
    advance(1)
    forward(7)
    forward(1)
    docs_event(0)
    take_in(0)
    for copy in passed:
        copy.wait_recv()
    got_table = here(tblx, sm_got, 7)
    advance(2)
    docs_event(1)
    forward(6)
    forward(2)
    take_in(7)
    take_in(1)
    docs_event(2)
    advance(3)
    forward(5)
    forward(3)
    docs_event(3)
    rope_up.wait_recv()
    span = rope(h_down, 0, DOC_DEV // 2)
    pass_up[2] = remote(span, span, ys.at[0, 7], yr.at[0, 7], up)
    cross(rope(h_down))
    rope_down.wait_recv()
    span = rope(h_up, DOC_DEV // 2, DOC_DEV // 2)
    pass_down[2] = remote(span, span, ys.at[1, 7], yr.at[1, 7], down)
    cross(rope(h_up))
    take_in(6)
    take_in(2)
    for k in range(CHUNKS):
        hops[k * 2 // CHUNKS, 3, k].wait_recv()
    forward(4)
    take_in(5)
    take_in(3)
    for e in range(CHUNKS // 2):
        pass_up[e].wait_recv()
        cross(lat(h_far, e * part, part))
        pass_down[e].wait_recv()
        cross(lat(h_far, (e + 2) * part, part))
    take_in(4)
    pass_up[2].wait_recv()
    cross(rope(h_far, 0, DOC_DEV // 2))
    pass_down[2].wait_recv()
    cross(rope(h_far, DOC_DEV // 2, DOC_DEV // 2))
    own_lat.wait()
    own_table.wait()
    got_table.wait()
    for copy in crossed:
        copy.wait_recv()

    attend(4)
    attend(3)
    settle(4, None, [(0, 3, low, pl.ds(0, 1), right), (1, 5, high, pl.ds(1, 1), left)])
    attend(5)
    settle(3, 0, [(2, 2, everything, both, right)])
    attend(2)
    settle(5, 1, [(3, 6, everything, both, left)])
    attend(6)
    settle(2, 2, [(4, 1, everything, both, right)])
    attend(1)
    settle(6, 3, [(5, 7, everything, both, left)])
    attend(7)
    settle(1, 4, [(6, 0, everything, both, right)])
    attend(0)
    settle(7, 5, [(7, 4, everything, both, left)])

    def own_values(p, at):
        return vals[OWN, p, :, :, at : at + VDIM].reshape(TOK, VDIM)

    def last_ready(p):
        falling_v[6, p].wait_recv()
        falling_v[7, p].wait_recv()

    def store(p, at, values):
        first = p * (VW // HALVES) + at
        out_ref[:, first : first + VDIM] = values

    def done(_):
        return None

    falling_l[6].wait_recv()
    falling_l[7].wait_recv()
    merge(
        0, [incoming(0), incoming(4), (own_values, lses[OWN].reshape(REQ, TOK))],
        done, last_ready, store, done,
    )
    for copy in sent:
        copy.wait_send()


def whole(q_nope, q_rope, latent_turned, doc_cache, w_uk, w_uv, doc_slot, doc_blocks, pair_doc, pair_req):
    local = pl.BlockSpec(memory_space=pltpu.VMEM)
    anywhere = pl.BlockSpec(memory_space=pl.ANY)
    scalar = pl.BlockSpec(memory_space=pltpu.SMEM)
    dma = pltpu.SemaphoreType.DMA
    return pl.pallas_call(
        whole_kernel,
        out_shape=jax.ShapeDtypeStruct((TOK, VW), BF16),
        in_specs=[anywhere, anywhere, local, anywhere, anywhere, anywhere] + [scalar] * 4,
        out_specs=local,
        scratch_shapes=[
            pltpu.VMEM((DOC_DEV, 2, HD, POS // 2, RANK), BF16),
            pltpu.VMEM((DOC_DEV, HD, POS // 2, LANES), BF16),
            pltpu.VMEM((DOC_DEV, 2, POS // 2, LATENT), BF16),
            pltpu.VMEM((HD, NOPE, RANK), BF16),
            pltpu.VMEM((HD, RANK, VDIM), BF16),
            pltpu.VMEM((TOK, LATENT), BF16),
            pltpu.VMEM((NZ, TOK, QW), BF16),
            pltpu.VMEM((NZ, NX, ROWS, QW), BF16),
            pltpu.VMEM((NZ, NX, ROWS, QW), BF16),
            pltpu.VMEM((NZ, 1, TBL), jnp.int32),
            pltpu.VMEM((NZ, 1, TBL), jnp.int32),
            pltpu.VMEM((NX, NZ, 1, TBL), jnp.int32),
            pltpu.SMEM((NZ, 1, TBL), jnp.int32),
            pltpu.SMEM((NX, NZ, 1, TBL), jnp.int32),
            pltpu.VMEM(((NZ + 1) * GROUP, HD, Q_LEN, RANK), BF16),
            pltpu.VMEM(((NZ + 1) * GROUP, HD, Q_LEN, LANES), BF16),
            pltpu.VMEM(((NZ + 1) * GROUP, HD, Q_LEN, LANES), BF16),
            pltpu.VMEM((GROUP, HD, Q_LEN, VDIM), F32),
            pltpu.VMEM((NZ + 1, HALVES, NX, ROWS, VW // HALVES), BF16),
            pltpu.VMEM((NZ + 1, NX, CAP, TOK), F32),
            pltpu.VMEM((NZ, HALVES, NX, ROWS, VW // HALVES), BF16),
            pltpu.VMEM((NZ, NX, CAP, TOK), F32),
            pltpu.VMEM((NZ, HALVES, TOK, VW // HALVES), BF16),
            pltpu.VMEM((NZ, 2, REQ // 2, TOK), F32),
            pltpu.VMEM((NZ, HALVES, TOK, VW // HALVES), BF16),
            pltpu.VMEM((NZ, 2, REQ // 2, TOK), F32),
            dma((2, 4, CHUNKS)), dma((2, 4, CHUNKS)),
            dma((NZ,)), dma((NZ,)),
            dma((NX,)), dma((NX,)),
            dma((NZ, NX)), dma((NZ, NX)),
            dma((2, 8)), dma((2, 8)),
            dma((18,)), dma((18,)),
            dma((NZ, HALVES, NX)), dma((NZ, HALVES, NX)),
            dma((NZ, NX)), dma((NZ, NX)),
            dma((8, HALVES)), dma((8, HALVES)),
            dma((8,)), dma((8,)),
            dma((8,)),
        ],
        compiler_params=pltpu.CompilerParams(
            collective_id=0, has_side_effects=True, vmem_limit_bytes=VMEM_LIMIT
        ),
        name="whole",
    )(q_nope, q_rope, latent_turned, doc_cache, w_uk, w_uv, doc_slot, doc_blocks, pair_doc, pair_req)


def on_device(
    q_nope, q_rope, question_latent, doc_cache, w_uk, w_uv, doc_slot, doc_blocks, pair_doc, pair_req
):
    return whole(
        q_nope, q_rope, question_latent.T, doc_cache.reshape(DOC_DEV, 2, POS // 2, LATENT),
        w_uk, w_uv, doc_slot, doc_blocks, pair_doc, pair_req,
    )


def solution(mesh):
    placed = (
        P("doc", "head"),
        P("doc", "head"),
        P("doc", None),
        P("doc", "head", None),
        P("head", None, None),
        P("head", None, None),
        P(),
        P(),
        P("doc"),
        P("doc"),
    )
    return jax.shard_map(
        on_device, mesh=mesh, in_specs=placed, out_specs=P("doc", "head"), check_vma=False
    )
```

time: 119 us -> 107 us (0.90)
  Pallas kernels: 111 us -> 104 us
  local copies, waits for them, and re-layouts: 4.37 us -> 1.67 us
  other arithmetic: 2.49 us -> 0 us
    pallas_call x1, Pallas kernels: 111 us -> 104 us  [whole(): pl.pallas_call(whole_kernel, out_shape=jax.ShapeDtypeStruct((TOK, VW), BF...]
    unnamed x2 -> x1, local copies, waits for them, and re-layouts: 3.38 us -> 1.67 us
where the time goes in v3:
time: 107 us; the launch traced here: 106 us
  Pallas kernels  104 us (97%)
  local copies, waits for them, and re-layouts  1.67 us (2%)
    pallas_call x1, Pallas kernels, whole(): pl.pallas_call(whole_kernel, out_shape=jax.ShapeDtypeStruct((TOK, VW), BF...  104 us

profile of v3, /device:TPU:4, one launch (start us, length us, event | category | flops | bytes accessed | tf_op | source)
XLA Modules:
  0.0 105.7 jit_solution(1987751704276226943)
XLA Ops:
  0.0 104.0 %whole.1 = bf16[128,1024]{1,0:T(8,128)(2,1)} custom-call(bf16[128,1024]{1,0:T(8,128)(2,1)} %qn_ref.1, bf16[128,512]{1,0:T(8,128)(2,1)} %qr_ref.1, bf16[576,128]{1,0:T(8,128)(2,1)} %bitcast.3, bf16[16,2,32,576]{3,2,1,0:T(8,128)(2,1)} %bitcast.2, bf16[8,128,512]{2,1,0:T(8,128)(2,1)} %uk_hbm.1, bf16[8,512,128]{2,1,0:T(8,128)(2,1)} %uv_hbm.1, s32[512]{0:T(512)} %slot_ref.1, ...), custom_call_target="tpu_custom_call" | custom-call | tf_op jit(solution)/shard_map/whole/pallas_call | solution.py:520
  104.0 1.7 %copy.12 = bf16[128,1024]{1,0:T(8,128)(2,1)} copy(bf16[128,1024]{1,0:T(8,128)(2,1)} %whole.1) | data formatting | bytes 524288

commit v4 on v3

--- a/solution.py
+++ b/solution.py
@@ -26,6 +26,8 @@
 GROUP = NX * CAP
 CHUNKS = 4
 HALVES = 2
+QUARTERS = 4
+VQ = HD * VDIM // QUARTERS
 OWN = NZ
 NW = HD * NOPE
 QW = HD * (NOPE + ROPE)
@@ -40,7 +42,7 @@
 MESH = pl.DeviceIdType.MESH
 F32 = jnp.float32
 BF16 = jnp.bfloat16
-VMEM_LIMIT = 58 * 1024 * 1024
+VMEM_LIMIT = 62 * 1024 * 1024
 
 
 def dot(a, b, dims):
@@ -49,8 +51,8 @@
 
 def whole_kernel(
     qn_ref, qr_ref, qlt_ref, doc_ref, uk_hbm, uv_hbm, slot_ref, blocks_ref, name_ref, request_ref, out_ref,
-    full_lat, full_rope, doc_in, uk_ref, uv_ref, ql, gq, sendb, slots, tbl, tblb, tblx, sm_own, sm_got,
-    qa, q_lo, q_hi, inv, vals, lses, xv, xl, pv, plse, in_v, in_l,
+    full_lat, full_rope, kt, doc_in, uk_ref, uv_ref, ql, gq, sendb, slots, tbl, tblb, tblx, sm_own, sm_got,
+    qa, q_rope, inv, vals, lses, xv, xl, pv, plse, in_v, in_l,
     zs, zr, ts, tr, us, ur, xs, xr, ys, yr, cs, cr, vs, vr, es, er, ps, pr, fs, fr, ls,
 ):
     d = lax.axis_index("doc")
@@ -78,10 +80,10 @@
     doc_lat = doc_ref.at[:, :, :, pl.ds(0, RANK)]
 
     def lat(head, first=0, count=DOC_DEV):
-        return full_lat.at[pl.ds(first, count), :, head]
+        return full_lat.at[pl.ds(first, count), head // 2, :, head % 2]
 
     def rope(head, first=0, count=DOC_DEV):
-        return full_rope.at[pl.ds(first, count), head]
+        return full_rope.at[pl.ds(first, count), head // 2, head % 2]
 
     queries_in = [
         here(qn_ref, gq.at[0, :, pl.ds(0, NW)], 0),
@@ -90,59 +92,6 @@
     docs_in = here(doc_ref, doc_in, 2)
     own_lat = here(doc_lat, lat(h), 3)
     weights_in = [here(uk_hbm, uk_ref, 4), here(uv_hbm, uv_ref, 5)]
-    for copy in queries_in:
-        copy.wait()
-    pl.semaphore_wait(barrier, len(greeted))
-
-    sent = []
-
-    def remote(src, dst, send, recv, peer):
-        copy = pltpu.make_async_remote_copy(
-            src_ref=src, dst_ref=dst, send_sem=send, recv_sem=recv, device_id=peer, device_id_type=MESH
-        )
-        copy.start()
-        sent.append(copy)
-        return copy
-
-    half = TOK // 2
-    low, high = pl.ds(0, half), pl.ds(half, half)
-    chain = ((0, 7, 6, 5, 4), (0, 1, 2, 3, 4))
-    hops = {}
-
-    def hop(way, step, k):
-        rows = pl.ds(k * (TOK // CHUNKS), TOK // CHUNKS)
-        hops[way, step, k] = remote(
-            gq.at[chain[way][step], rows], gq.at[chain[way][step + 1], rows],
-            zs.at[way, step, k], zr.at[way, step, k], (right, left)[way],
-        )
-
-    for k in range(CHUNKS):
-        hop(0, 0, k)
-        hop(1, 0, k)
-
-    def advance(step):
-        for k in range(CHUNKS):
-            for way in range(2):
-                hops[way, step - 1, k].wait_recv()
-                if step < 3 or (k < CHUNKS // 2) == (way == 0):
-                    hop(way, step, k)
-
-    part = DOC_DEV // CHUNKS
-    docs_up, docs_down, pass_up, pass_down, crossed = {}, {}, {}, {}, []
-
-    def cross(src):
-        i = len(crossed)
-        crossed.append(remote(src, src, cs.at[i], cr.at[i], other))
-
-    def doc_part(k):
-        return doc_ref.at[pl.ds(k * part, part), :, :, pl.ds(0, RANK)]
-
-    for e in range(CHUNKS):
-        k, m = e, (e + 2) % CHUNKS
-        docs_up[k] = remote(doc_part(k), lat(h, k * part, part), ys.at[0, k], yr.at[0, k], up)
-        docs_down[m] = remote(doc_part(m), lat(h, m * part, part), ys.at[1, m], yr.at[1, m], down)
-    crossed.append(remote(doc_lat, lat(h), cs.at[0], cr.at[0], other))
-
     lane = lax.broadcasted_iota(jnp.int32, (NZ, TOK), 1)
     channel = lax.broadcasted_iota(jnp.int32, (NZ, TOK), 0) * NX + lane // ROWS
     turn_at = (lane % ROWS) // Q_LEN
@@ -165,6 +114,59 @@
     routed = lax.fori_loop(0, PAIRS, route, (nothing - 1, nothing, nothing, nothing))
     for k in range(3):
         tbl[:, :, k * TOK : (k + 1) * TOK] = routed[k].reshape(NZ, 1, TOK)
+    for copy in queries_in:
+        copy.wait()
+    pl.semaphore_wait(barrier, len(greeted))
+
+    sent = []
+
+    def remote(src, dst, send, recv, peer):
+        copy = pltpu.make_async_remote_copy(
+            src_ref=src, dst_ref=dst, send_sem=send, recv_sem=recv, device_id=peer, device_id_type=MESH
+        )
+        copy.start()
+        sent.append(copy)
+        return copy
+
+    half = TOK // 2
+    low, high = pl.ds(0, half), pl.ds(half, half)
+    chain = ((0, 7, 6, 5, 4), (0, 1, 2, 3, 4))
+    hops = {}
+
+    def hop(way, step, k):
+        rows = pl.ds(k * (TOK // CHUNKS), TOK // CHUNKS)
+        hops[way, step, k] = remote(
+            gq.at[chain[way][step], rows], gq.at[chain[way][step + 1], rows],
+            zs.at[way, step, k], zr.at[way, step, k], (right, left)[way],
+        )
+
+    for k in range(CHUNKS):
+        hop(0, 0, k)
+        hop(1, 0, k)
+
+    def advance(step):
+        for k in range(CHUNKS):
+            for way in range(2):
+                hops[way, step - 1, k].wait_recv()
+                if step < 3 or (k < CHUNKS // 2) == (way == 0):
+                    hop(way, step, k)
+
+    part = DOC_DEV // CHUNKS
+    docs_up, docs_down, pass_up, pass_down, crossed = {}, {}, {}, {}, []
+
+    def cross(src):
+        i = len(crossed)
+        crossed.append(remote(src, src, cs.at[i], cr.at[i], other))
+
+    def doc_part(k):
+        return doc_ref.at[pl.ds(k * part, part), :, :, pl.ds(0, RANK)]
+
+    for e in range(CHUNKS):
+        k, m = e, (e + 2) % CHUNKS
+        docs_up[k] = remote(doc_part(k), lat(h, k * part, part), ys.at[0, k], yr.at[0, k], up)
+        docs_down[m] = remote(doc_part(m), lat(h, m * part, part), ys.at[1, m], yr.at[1, m], down)
+    crossed.append(remote(doc_lat, lat(h), cs.at[0], cr.at[0], other))
+
     tables = [
         remote(tbl.at[(z + j) % NZ], tblb.at[z], ts.at[j], tr.at[j], z_peer[j]) for j in range(1, NZ)
     ]
@@ -172,7 +174,7 @@
 
     docs_in.wait()
     packed = jnp.concatenate([doc_in[:, 0, :, RANK:LATENT], doc_in[:, 1, :, RANK:LATENT]], axis=2)
-    full_rope[:, pl.ds(h, 1)] = packed.reshape(DOC_DEV, 1, POS // 2, LANES)
+    full_rope[:, pl.ds(y, 1), pl.ds(c, 1)] = packed.reshape(DOC_DEV, 1, 1, POS // 2, LANES)
     rope_up = remote(rope(h), rope(h), ys.at[0, 4], yr.at[0, 4], up)
     rope_down = remote(rope(h), rope(h), ys.at[1, 4], yr.at[1, 4], down)
     cross(rope(h))
@@ -205,14 +207,11 @@
 
     def absorb(group, rows):
         span = pl.ds(group * GROUP, GROUP)
-        blank = jnp.zeros((TOK, ROPE), BF16)
         for head in range(HD):
             nope = rows(head * NOPE, NOPE).reshape(TOK, NOPE)
             absorbed = dot(nope, uk_ref[head], ((1,), (0,))).astype(BF16)
             qa[span, head] = absorbed.reshape(GROUP, Q_LEN, RANK)
-            turned = rows(NW + head * ROPE, ROPE).reshape(TOK, ROPE)
-            q_lo[span, head] = jnp.concatenate([turned, blank], axis=1).reshape(GROUP, Q_LEN, LANES)
-            q_hi[span, head] = jnp.concatenate([blank, turned], axis=1).reshape(GROUP, Q_LEN, LANES)
+            q_rope[span, head] = rows(NW + head * ROPE, ROPE).reshape(GROUP, Q_LEN, ROPE)
 
     def take_in(rel):
         for copy in arriving[rel]:
@@ -256,9 +255,8 @@
             slot = OWN * GROUP + r
             keys = ql[r * Q_LEN : (r + 1) * Q_LEN, 0:RANK]
             rope_k = ql[r * Q_LEN : (r + 1) * Q_LEN, RANK:LATENT]
-            turned = q_lo[slot].reshape(TOK, LANES)[:, 0:ROPE]
             scores = dot(qa[slot].reshape(TOK, RANK), keys, ((1,), (1,))) + dot(
-                turned, rope_k, ((1,), (1,))
+                q_rope[slot].reshape(TOK, ROPE), rope_k, ((1,), (1,))
             )
             weights, scale, as_row = softmax(jnp.where(key_at <= query_at, scores, LOWEST))
             lses[OWN, r // CAP, r % CAP : r % CAP + 1] = as_row
@@ -266,41 +264,40 @@
         for p in range(HALVES):
             project(OWN, p)
 
-    key_block = lax.broadcasted_iota(jnp.int32, (1, DOC_LEN), 1) % (DOC_LEN // 2) // (BLOCK // 2)
+    def turn(block):
+        columns = pl.ds(pl.multiple_of(block * BLOCK, BLOCK), BLOCK)
+
+        def one_doc(doc, carry):
+            kt[doc, 0:RANK, columns] = jnp.transpose(full_lat[doc, block].reshape(BLOCK, RANK))
+            turned = jnp.transpose(full_rope[doc, block].reshape(POS, LANES).astype(F32)).astype(BF16)
+            kt[doc, RANK:LATENT, columns] = jnp.concatenate([turned[0:ROPE], turned[ROPE:LANES]], axis=1)
+            return carry
+
+        lax.fori_loop(0, DOC_DEV, one_doc, 0)
+
+    key_block = lax.broadcasted_iota(jnp.int32, (1, DOC_LEN), 1) // BLOCK
     returning = {}
 
     def attend(rel):
         owner = (z + rel) % NZ
-
-        def quad(g, carry):
-            jobs = []
-            for i in range(4):
-                source, turn = g * 2 + i // CAP, i % CAP
-                first = x * ROWS + turn * Q_LEN
-                doc = sm_got[source, owner, 0, TOK + first]
-                blocks = sm_got[source, owner, 0, 2 * TOK + first]
-                index = g * 4 + i
-                slot = rel * GROUP + index
-                keys = full_lat[doc].reshape(DOC_LEN, RANK)
-                turned = full_rope[doc].reshape(DOC_LEN // 2, LANES)
-                scores = dot(qa[slot].reshape(TOK, RANK), keys, ((1,), (1,))) + jnp.concatenate(
-                    [
-                        dot(q_lo[slot].reshape(TOK, LANES), turned, ((1,), (1,))),
-                        dot(q_hi[slot].reshape(TOK, LANES), turned, ((1,), (1,))),
-                    ],
-                    axis=1,
-                )
-                jobs.append((source, turn, doc, blocks, index, slot, scores))
-            soft = []
-            for source, turn, doc, blocks, index, slot, scores in jobs:
-                hide = jnp.where(key_block < blocks, 0.0, LOWEST)
-                soft.append(softmax(scores + hide))
-            for (source, turn, doc, blocks, index, slot, scores), (weights, scale, as_row) in zip(jobs, soft):
-                lses[rel, source, turn : turn + 1] = as_row
-                finish(slot, index, weights, scale, full_lat[doc].reshape(DOC_LEN, RANK))
-            return carry
-
-        lax.fori_loop(0, GROUP // 4, quad, 0)
+        jobs = []
+        for index in range(GROUP):
+            source, turn_of = index // CAP, index % CAP
+            first = x * ROWS + turn_of * Q_LEN
+            doc = sm_got[source, owner, 0, TOK + first]
+            blocks = sm_got[source, owner, 0, 2 * TOK + first]
+            slot = rel * GROUP + index
+            scores = dot(qa[slot].reshape(TOK, RANK), kt[doc, 0:RANK], ((1,), (0,))) + dot(
+                q_rope[slot].reshape(TOK, ROPE), kt[doc, RANK:LATENT], ((1,), (0,))
+            )
+            jobs.append((source, turn_of, doc, blocks, index, slot, scores))
+        soft = []
+        for source, turn_of, doc, blocks, index, slot, scores in jobs:
+            hide = jnp.where(key_block < blocks, 0.0, LOWEST)
+            soft.append(softmax(scores + hide))
+        for (source, turn_of, doc, blocks, index, slot, scores), (weights, scale, as_row) in zip(jobs, soft):
+            lses[rel, source, turn_of : turn_of + 1] = as_row
+            finish(slot, index, weights, scale, full_lat[doc].reshape(DOC_LEN, RANK))
         returning[rel] = [
             [
                 remote(lses.at[rel, (x + j) % NX], xl.at[rel, x], es.at[rel, j], er.at[rel, j], x_peer[j])
@@ -323,7 +320,7 @@
 
     request_at = lax.broadcasted_iota(jnp.int32, (REQ, TOK), 0) * Q_LEN
 
-    def merge(rel, partials, lse_done, half_ready, store, half_done):
+    def merge(rel, partials, lse_done, part_ready, store, part_done):
         owner = (z + rel) % NZ
         pick = picked(rel)
         for copy in returning[rel][0]:
@@ -350,9 +347,11 @@
         for p in range(HALVES):
             for copy in returning[rel][1 + p]:
                 copy.wait_recv()
-            half_ready(p)
             for j in range(HD // HALVES):
                 head = p * (HD // HALVES) + j
+                quarter, at_quarter = head // 2, head % 2 * VDIM
+                if head % 2 == 0:
+                    part_ready(quarter)
                 mine = turned[head * Q_LEN : (head + 1) * Q_LEN]
 
                 def stacked(first):
@@ -363,12 +362,16 @@
                 scaled = (slot_values * stacked(count * REQ)).astype(BF16)
                 result = dot(pick, scaled, ((1,), (0,)))
                 for k, (values, _) in enumerate(partials):
-                    result = result + values(p, at).astype(F32) * stacked(k * REQ)
-                store(p, at, result.astype(BF16))
-            half_done(p)
+                    result = result + values(head).astype(F32) * stacked(k * REQ)
+                store(quarter, at_quarter, result.astype(BF16))
+                if head % 2 == 1:
+                    part_done(quarter)
 
     def incoming(i):
-        return (lambda p, at: in_v[i, p, :, at : at + VDIM]), in_l[i].reshape(REQ, TOK)
+        def values(head):
+            return in_v[i, head // 2, :, head % 2 * VDIM : (head % 2 + 1) * VDIM]
+
+        return values, in_l[i].reshape(REQ, TOK)
 
     falling_l, falling_v = {}, {}
     everything, both = pl.ds(0, TOK), pl.ds(0, 2)
@@ -381,14 +384,14 @@
                     plse.at[rel, span_l], in_l.at[target, span_l], fs.at[i], fr.at[i], peer
                 )
 
-        def half_ready(p):
+        def part_ready(p):
             if awaited is not None:
                 falling_v[awaited, p].wait_recv()
 
         def store(p, at, values):
             pv[rel, p, :, at : at + VDIM] = values
 
-        def half_done(p):
+        def part_done(p):
             for i, target, span, span_l, peer in moves:
                 falling_v[i, p] = remote(
                     pv.at[rel, p, span], in_v.at[target, p, span], ps.at[i, p], pr.at[i, p], peer
@@ -398,10 +401,10 @@
         if awaited is not None:
             falling_l[awaited].wait_recv()
             partials = [incoming(rel)]
-        merge(rel, partials, lse_done, half_ready, store, half_done)
-
-    in_v[3, :, half:TOK] = jnp.zeros((HALVES, half, VW // HALVES), BF16)
-    in_v[5, :, 0:half] = jnp.zeros((HALVES, half, VW // HALVES), BF16)
+        merge(rel, partials, lse_done, part_ready, store, part_done)
+
+    in_v[3, :, half:TOK] = jnp.zeros((QUARTERS, half, VQ), BF16)
+    in_v[5, :, 0:half] = jnp.zeros((QUARTERS, half, VQ), BF16)
     in_l[3, 1] = jnp.full((REQ // 2, TOK), LOWEST, F32)
     in_l[5, 0] = jnp.full((REQ // 2, TOK), LOWEST, F32)
 
@@ -425,21 +428,25 @@
     advance(1)
     forward(7)
     forward(1)
-    docs_event(0)
     take_in(0)
     for copy in passed:
         copy.wait_recv()
     got_table = here(tblx, sm_got, 7)
+    own_lat.wait()
+    for copy in crossed[0:2]:
+        copy.wait_recv()
+    turn(y)
     advance(2)
-    docs_event(1)
     forward(6)
     forward(2)
     take_in(7)
     take_in(1)
-    docs_event(2)
+    docs_event(0)
+    docs_event(1)
     advance(3)
     forward(5)
     forward(3)
+    docs_event(2)
     docs_event(3)
     rope_up.wait_recv()
     span = rope(h_down, 0, DOC_DEV // 2)
@@ -454,6 +461,10 @@
     for k in range(CHUNKS):
         hops[k * 2 // CHUNKS, 3, k].wait_recv()
     forward(4)
+    for copy in crossed[2:12]:
+        copy.wait_recv()
+    turn((y + 1) % NY)
+    turn((y + NY - 1) % NY)
     take_in(5)
     take_in(3)
     for e in range(CHUNKS // 2):
@@ -461,16 +472,16 @@
         cross(lat(h_far, e * part, part))
         pass_down[e].wait_recv()
         cross(lat(h_far, (e + 2) * part, part))
-    take_in(4)
     pass_up[2].wait_recv()
     cross(rope(h_far, 0, DOC_DEV // 2))
     pass_down[2].wait_recv()
     cross(rope(h_far, DOC_DEV // 2, DOC_DEV // 2))
-    own_lat.wait()
     own_table.wait()
     got_table.wait()
-    for copy in crossed:
+    take_in(4)
+    for copy in crossed[12:]:
         copy.wait_recv()
+    turn((y + 2) % NY)
 
     attend(4)
     attend(3)
@@ -488,15 +499,16 @@
     attend(0)
     settle(7, 5, [(7, 4, everything, both, left)])
 
-    def own_values(p, at):
-        return vals[OWN, p, :, :, at : at + VDIM].reshape(TOK, VDIM)
+    def own_values(head):
+        at = head % (HD // HALVES) * VDIM
+        return vals[OWN, head // (HD // HALVES), :, :, at : at + VDIM].reshape(TOK, VDIM)
 
     def last_ready(p):
         falling_v[6, p].wait_recv()
         falling_v[7, p].wait_recv()
 
     def store(p, at, values):
-        first = p * (VW // HALVES) + at
+        first = p * VQ + at
         out_ref[:, first : first + VDIM] = values
 
     def done(_):
@@ -523,8 +535,9 @@
         in_specs=[anywhere, anywhere, local, anywhere, anywhere, anywhere] + [scalar] * 4,
         out_specs=local,
         scratch_shapes=[
-            pltpu.VMEM((DOC_DEV, 2, HD, POS // 2, RANK), BF16),
-            pltpu.VMEM((DOC_DEV, HD, POS // 2, LANES), BF16),
+            pltpu.VMEM((DOC_DEV, NY, 2, 2, POS // 2, RANK), BF16),
+            pltpu.VMEM((DOC_DEV, NY, 2, POS // 2, LANES), BF16),
+            pltpu.VMEM((DOC_DEV, LATENT, DOC_LEN), BF16),
             pltpu.VMEM((DOC_DEV, 2, POS // 2, LATENT), BF16),
             pltpu.VMEM((HD, NOPE, RANK), BF16),
             pltpu.VMEM((HD, RANK, VDIM), BF16),
@@ -538,16 +551,15 @@
             pltpu.SMEM((NZ, 1, TBL), jnp.int32),
             pltpu.SMEM((NX, NZ, 1, TBL), jnp.int32),
             pltpu.VMEM(((NZ + 1) * GROUP, HD, Q_LEN, RANK), BF16),
-            pltpu.VMEM(((NZ + 1) * GROUP, HD, Q_LEN, LANES), BF16),
-            pltpu.VMEM(((NZ + 1) * GROUP, HD, Q_LEN, LANES), BF16),
+            pltpu.VMEM(((NZ + 1) * GROUP, HD, Q_LEN, ROPE), BF16),
             pltpu.VMEM((GROUP, HD, Q_LEN, VDIM), F32),
             pltpu.VMEM((NZ + 1, HALVES, NX, ROWS, VW // HALVES), BF16),
             pltpu.VMEM((NZ + 1, NX, CAP, TOK), F32),
             pltpu.VMEM((NZ, HALVES, NX, ROWS, VW // HALVES), BF16),
             pltpu.VMEM((NZ, NX, CAP, TOK), F32),
-            pltpu.VMEM((NZ, HALVES, TOK, VW // HALVES), BF16),
+            pltpu.VMEM((NZ, QUARTERS, TOK, VQ), BF16),
             pltpu.VMEM((NZ, 2, REQ // 2, TOK), F32),
-            pltpu.VMEM((NZ, HALVES, TOK, VW // HALVES), BF16),
+            pltpu.VMEM((NZ, QUARTERS, TOK, VQ), BF16),
             pltpu.VMEM((NZ, 2, REQ // 2, TOK), F32),
             dma((2, 4, CHUNKS)), dma((2, 4, CHUNKS)),
             dma((NZ,)), dma((NZ,)),
@@ -557,7 +569,7 @@
             dma((18,)), dma((18,)),
             dma((NZ, HALVES, NX)), dma((NZ, HALVES, NX)),
             dma((NZ, NX)), dma((NZ, NX)),
-            dma((8, HALVES)), dma((8, HALVES)),
+            dma((8, QUARTERS)), dma((8, QUARTERS)),
             dma((8,)), dma((8,)),
             dma((8,)),
         ],

time: 107 us -> 106 us (level)
    pallas_call x1, Pallas kernels: 104 us -> 103 us  [whole(): pl.pallas_call(whole_kernel, out_shape=jax.ShapeDtypeStruct((TOK, VW), BF...]
where the time goes in v4:
time: 106 us; the launch traced here: 105 us
  Pallas kernels  103 us (97%)
  local copies, waits for them, and re-layouts  1.67 us (2%)
    pallas_call x1, Pallas kernels, whole(): pl.pallas_call(whole_kernel, out_shape=jax.ShapeDtypeStruct((TOK, VW), BF...  103 us

profile of v4, /device:TPU:4, one launch (start us, length us, event | category | flops | bytes accessed | tf_op | source)
XLA Modules:
  0.0 104.5 jit_solution(2760928306231957472)
XLA Ops:
  0.0 102.9 %whole.1 = bf16[128,1024]{1,0:T(8,128)(2,1)} custom-call(bf16[128,1024]{1,0:T(8,128)(2,1)} %qn_ref.1, bf16[128,512]{1,0:T(8,128)(2,1)} %qr_ref.1, bf16[576,128]{1,0:T(8,128)(2,1)} %bitcast.3, bf16[16,2,32,576]{3,2,1,0:T(8,128)(2,1)} %bitcast.2, bf16[8,128,512]{2,1,0:T(8,128)(2,1)} %uk_hbm.1, bf16[8,512,128]{2,1,0:T(8,128)(2,1)} %uv_hbm.1, s32[512]{0:T(512)} %slot_ref.1, ...), custom_call_target="tpu_custom_call" | custom-call | tf_op jit(solution)/shard_map/whole/pallas_call | solution.py:532
  102.9 1.7 %copy.12 = bf16[128,1024]{1,0:T(8,128)(2,1)} copy(bf16[128,1024]{1,0:T(8,128)(2,1)} %whole.1) | data formatting | bytes 524288

commit v5 on v4

--- a/solution.py
+++ b/solution.py
@@ -161,10 +161,13 @@
     def doc_part(k):
         return doc_ref.at[pl.ds(k * part, part), :, :, pl.ds(0, RANK)]
 
-    for e in range(CHUNKS):
+    def send_docs(e):
         k, m = e, (e + 2) % CHUNKS
         docs_up[k] = remote(doc_part(k), lat(h, k * part, part), ys.at[0, k], yr.at[0, k], up)
         docs_down[m] = remote(doc_part(m), lat(h, m * part, part), ys.at[1, m], yr.at[1, m], down)
+
+    send_docs(0)
+    send_docs(1)
     crossed.append(remote(doc_lat, lat(h), cs.at[0], cr.at[0], other))
 
     tables = [
@@ -178,12 +181,6 @@
     rope_up = remote(rope(h), rope(h), ys.at[0, 4], yr.at[0, 4], up)
     rope_down = remote(rope(h), rope(h), ys.at[1, 4], yr.at[1, 4], down)
     cross(rope(h))
-
-    for copy in tables:
-        copy.wait_recv()
-    passed = [remote(tblb, tblx.at[x], us.at[j], ur.at[j], x_peer[j]) for j in range(1, NX)]
-    tblx[pl.ds(x, 1)] = tblb[...].reshape(1, NZ, 1, TBL)
-    own_table = here(tblb, sm_own, 6)
 
     token = lax.broadcasted_iota(jnp.int32, (TOK, NX * ROWS), 0)
     arriving = {}
@@ -244,14 +241,16 @@
                 NX, ROWS, VDIM
             )
 
-    def own_term():
+    def own_start():
         for k in range(0, LATENT, LANES):
             width = min(LANES, LATENT - k)
             ql[:, k : k + width] = jnp.transpose(qlt_ref[k : k + width].astype(F32)).astype(BF16)
         absorb(OWN, lambda first, width: gq[0, :, first : first + width])
+
+    def own_part(requests):
         key_at = lax.broadcasted_iota(jnp.int32, (TOK, Q_LEN), 1)
         query_at = lax.broadcasted_iota(jnp.int32, (TOK, Q_LEN), 0) % Q_LEN
-        for r in range(REQ):
+        for r in requests:
             slot = OWN * GROUP + r
             keys = ql[r * Q_LEN : (r + 1) * Q_LEN, 0:RANK]
             rope_k = ql[r * Q_LEN : (r + 1) * Q_LEN, RANK:LATENT]
@@ -261,10 +260,8 @@
             weights, scale, as_row = softmax(jnp.where(key_at <= query_at, scores, LOWEST))
             lses[OWN, r // CAP, r % CAP : r % CAP + 1] = as_row
             finish(slot, r, weights, scale, keys)
-        for p in range(HALVES):
-            project(OWN, p)
-
-    def turn(block):
+
+    def turn(block, parts=((0, DOC_DEV),)):
         columns = pl.ds(pl.multiple_of(block * BLOCK, BLOCK), BLOCK)
 
         def one_doc(doc, carry):
@@ -273,7 +270,8 @@
             kt[doc, RANK:LATENT, columns] = jnp.concatenate([turned[0:ROPE], turned[ROPE:LANES]], axis=1)
             return carry
 
-        lax.fori_loop(0, DOC_DEV, one_doc, 0)
+        for first, last in parts:
+            lax.fori_loop(first, last, one_doc, 0)
 
     key_block = lax.broadcasted_iota(jnp.int32, (1, DOC_LEN), 1) // BLOCK
     returning = {}
@@ -422,32 +420,36 @@
         cross(lat(h_up, m * part, part))
 
     forward(0)
+    for copy in tables:
+        copy.wait_recv()
+    passed = [remote(tblb, tblx.at[x], us.at[j], ur.at[j], x_peer[j]) for j in range(1, NX)]
+    tblx[pl.ds(x, 1)] = tblb[...].reshape(1, NZ, 1, TBL)
+    own_table = here(tblb, sm_own, 6)
+    send_docs(2)
+    send_docs(3)
     for copy in weights_in:
         copy.wait()
-    own_term()
-    advance(1)
-    forward(7)
-    forward(1)
-    take_in(0)
-    for copy in passed:
-        copy.wait_recv()
-    got_table = here(tblx, sm_got, 7)
+    own_start()
+    own_part(range(0, REQ // 2))
     own_lat.wait()
     for copy in crossed[0:2]:
         copy.wait_recv()
     turn(y)
+    advance(1)
+    forward(7)
+    forward(1)
+    for copy in passed:
+        copy.wait_recv()
+    got_table = here(tblx, sm_got, 7)
+    docs_event(0)
+    docs_event(1)
+    own_part(range(REQ // 2, REQ))
+    for p in range(HALVES):
+        project(OWN, p)
+    take_in(0)
     advance(2)
     forward(6)
     forward(2)
-    take_in(7)
-    take_in(1)
-    docs_event(0)
-    docs_event(1)
-    advance(3)
-    forward(5)
-    forward(3)
-    docs_event(2)
-    docs_event(3)
     rope_up.wait_recv()
     span = rope(h_down, 0, DOC_DEV // 2)
     pass_up[2] = remote(span, span, ys.at[0, 7], yr.at[0, 7], up)
@@ -456,32 +458,45 @@
     span = rope(h_up, DOC_DEV // 2, DOC_DEV // 2)
     pass_down[2] = remote(span, span, ys.at[1, 7], yr.at[1, 7], down)
     cross(rope(h_up))
-    take_in(6)
-    take_in(2)
+    take_in(7)
+    take_in(1)
+    advance(3)
+    forward(5)
+    forward(3)
+    docs_event(2)
+    docs_event(3)
     for k in range(CHUNKS):
         hops[k * 2 // CHUNKS, 3, k].wait_recv()
     forward(4)
+    take_in(6)
+    take_in(2)
     for copy in crossed[2:12]:
         copy.wait_recv()
     turn((y + 1) % NY)
-    turn((y + NY - 1) % NY)
-    take_in(5)
-    take_in(3)
-    for e in range(CHUNKS // 2):
-        pass_up[e].wait_recv()
-        cross(lat(h_far, e * part, part))
-        pass_down[e].wait_recv()
-        cross(lat(h_far, (e + 2) * part, part))
     pass_up[2].wait_recv()
     cross(rope(h_far, 0, DOC_DEV // 2))
     pass_down[2].wait_recv()
     cross(rope(h_far, DOC_DEV // 2, DOC_DEV // 2))
+    pass_up[0].wait_recv()
+    cross(lat(h_far, 0, part))
+    pass_down[0].wait_recv()
+    cross(lat(h_far, 2 * part, part))
+    turn((y + NY - 1) % NY)
+    pass_up[1].wait_recv()
+    cross(lat(h_far, part, part))
+    pass_down[1].wait_recv()
+    cross(lat(h_far, 3 * part, part))
+    take_in(5)
+    take_in(3)
     own_table.wait()
     got_table.wait()
+    for copy in crossed[12:16]:
+        copy.wait_recv()
+    turn((y + 2) % NY, ((0, part), (2 * part, 3 * part)))
     take_in(4)
-    for copy in crossed[12:]:
+    for copy in crossed[16:]:
         copy.wait_recv()
-    turn((y + 2) % NY)
+    turn((y + 2) % NY, ((part, 2 * part), (3 * part, 4 * part)))
 
     attend(4)
     attend(3)

time: 106 us -> 105 us (level); the launches traced: 105 us -> 105 us
  no operation moved by 1% of the time
where the time goes in v5:
time: 105 us
  Pallas kernels  103 us (98%)
  local copies, waits for them, and re-layouts  1.67 us (2%)
    pallas_call x1, Pallas kernels, whole(): pl.pallas_call(whole_kernel, out_shape=jax.ShapeDtypeStruct((TOK, VW), BF...  103 us

profile of v5, /device:TPU:4, one launch (start us, length us, event | category | flops | bytes accessed | tf_op | source)
XLA Modules:
  0.0 104.7 jit_solution(1271016083703832133)
XLA Ops:
  0.0 103.0 %whole.1 = bf16[128,1024]{1,0:T(8,128)(2,1)} custom-call(bf16[128,1024]{1,0:T(8,128)(2,1)} %qn_ref.1, bf16[128,512]{1,0:T(8,128)(2,1)} %qr_ref.1, bf16[576,128]{1,0:T(8,128)(2,1)} %bitcast.3, bf16[16,2,32,576]{3,2,1,0:T(8,128)(2,1)} %bitcast.2, bf16[8,128,512]{2,1,0:T(8,128)(2,1)} %uk_hbm.1, bf16[8,512,128]{2,1,0:T(8,128)(2,1)} %uv_hbm.1, s32[512]{0:T(512)} %slot_ref.1, ...), custom_call_target="tpu_custom_call" | custom-call | tf_op jit(solution)/shard_map/whole/pallas_call | solution.py:547
  103.0 1.7 %copy.12 = bf16[128,1024]{1,0:T(8,128)(2,1)} copy(bf16[128,1024]{1,0:T(8,128)(2,1)} %whole.1) | data formatting | bytes 524288

commit v6 on v5

--- a/solution.py
+++ b/solution.py
@@ -266,7 +266,7 @@
 
         def one_doc(doc, carry):
             kt[doc, 0:RANK, columns] = jnp.transpose(full_lat[doc, block].reshape(BLOCK, RANK))
-            turned = jnp.transpose(full_rope[doc, block].reshape(POS, LANES).astype(F32)).astype(BF16)
+            turned = jnp.transpose(full_rope[doc, block].reshape(POS, LANES))
             kt[doc, RANK:LATENT, columns] = jnp.concatenate([turned[0:ROPE], turned[ROPE:LANES]], axis=1)
             return carry
 
@@ -430,7 +430,6 @@
     for copy in weights_in:
         copy.wait()
     own_start()
-    own_part(range(0, REQ // 2))
     own_lat.wait()
     for copy in crossed[0:2]:
         copy.wait_recv()
@@ -443,9 +442,6 @@
     got_table = here(tblx, sm_got, 7)
     docs_event(0)
     docs_event(1)
-    own_part(range(REQ // 2, REQ))
-    for p in range(HALVES):
-        project(OWN, p)
     take_in(0)
     advance(2)
     forward(6)
@@ -500,18 +496,21 @@
 
     attend(4)
     attend(3)
+    own_part(range(0, REQ))
+    for p in range(HALVES):
+        project(OWN, p)
     settle(4, None, [(0, 3, low, pl.ds(0, 1), right), (1, 5, high, pl.ds(1, 1), left)])
     attend(5)
+    attend(2)
     settle(3, 0, [(2, 2, everything, both, right)])
-    attend(2)
+    attend(6)
     settle(5, 1, [(3, 6, everything, both, left)])
-    attend(6)
+    attend(1)
     settle(2, 2, [(4, 1, everything, both, right)])
-    attend(1)
+    attend(7)
     settle(6, 3, [(5, 7, everything, both, left)])
-    attend(7)
+    attend(0)
     settle(1, 4, [(6, 0, everything, both, right)])
-    attend(0)
     settle(7, 5, [(7, 4, everything, both, left)])
 
     def own_values(head):

time: 105 us -> 102 us (0.971)
  Pallas kernels: 103 us -> 99.8 us
    pallas_call x1, Pallas kernels: 103 us -> 99.8 us  [whole(): pl.pallas_call(whole_kernel, out_shape=jax.ShapeDtypeStruct((TOK, VW), BF...]
where the time goes in v6:
time: 102 us; the launch traced here: 101 us
  Pallas kernels  99.8 us (98%)
  local copies, waits for them, and re-layouts  1.67 us (2%)
    pallas_call x1, Pallas kernels, whole(): pl.pallas_call(whole_kernel, out_shape=jax.ShapeDtypeStruct((TOK, VW), BF...  99.8 us

profile of v6, /device:TPU:4, one launch (start us, length us, event | category | flops | bytes accessed | tf_op | source)
XLA Modules:
  0.0 101.4 jit_solution(911539760654558081)
XLA Ops:
  0.0 99.8 %whole.1 = bf16[128,1024]{1,0:T(8,128)(2,1)} custom-call(bf16[128,1024]{1,0:T(8,128)(2,1)} %qn_ref.1, bf16[128,512]{1,0:T(8,128)(2,1)} %qr_ref.1, bf16[576,128]{1,0:T(8,128)(2,1)} %bitcast.3, bf16[16,2,32,576]{3,2,1,0:T(8,128)(2,1)} %bitcast.2, bf16[8,128,512]{2,1,0:T(8,128)(2,1)} %uk_hbm.1, bf16[8,512,128]{2,1,0:T(8,128)(2,1)} %uv_hbm.1, s32[512]{0:T(512)} %slot_ref.1, ...), custom_call_target="tpu_custom_call" | custom-call | tf_op jit(solution)/shard_map/whole/pallas_call | solution.py:546
  99.8 1.7 %copy.12 = bf16[128,1024]{1,0:T(8,128)(2,1)} copy(bf16[128,1024]{1,0:T(8,128)(2,1)} %whole.1) | data formatting | bytes 524288

commit v7 on v6

--- a/solution.py
+++ b/solution.py
@@ -503,12 +503,12 @@
     attend(5)
     attend(2)
     settle(3, 0, [(2, 2, everything, both, right)])
+    settle(5, 1, [(3, 6, everything, both, left)])
     attend(6)
-    settle(5, 1, [(3, 6, everything, both, left)])
     attend(1)
     settle(2, 2, [(4, 1, everything, both, right)])
+    settle(6, 3, [(5, 7, everything, both, left)])
     attend(7)
-    settle(6, 3, [(5, 7, everything, both, left)])
     attend(0)
     settle(1, 4, [(6, 0, everything, both, right)])
     settle(7, 5, [(7, 4, everything, both, left)])

time: 102 us -> 103 us (level)
  no operation moved by 1% of the time
where the time goes in v7:
time: 103 us; the launch traced here: 101 us
  Pallas kernels  99.8 us (97%)
  local copies, waits for them, and re-layouts  1.67 us (2%)
    pallas_call x1, Pallas kernels, whole(): pl.pallas_call(whole_kernel, out_shape=jax.ShapeDtypeStruct((TOK, VW), BF...  99.8 us

profile of v7, /device:TPU:4, one launch (start us, length us, event | category | flops | bytes accessed | tf_op | source)
XLA Modules:
  0.0 101.5 jit_solution(5245305980733254837)
XLA Ops:
  0.0 99.8 %whole.1 = bf16[128,1024]{1,0:T(8,128)(2,1)} custom-call(bf16[128,1024]{1,0:T(8,128)(2,1)} %qn_ref.1, bf16[128,512]{1,0:T(8,128)(2,1)} %qr_ref.1, bf16[576,128]{1,0:T(8,128)(2,1)} %bitcast.3, bf16[16,2,32,576]{3,2,1,0:T(8,128)(2,1)} %bitcast.2, bf16[8,128,512]{2,1,0:T(8,128)(2,1)} %uk_hbm.1, bf16[8,512,128]{2,1,0:T(8,128)(2,1)} %uv_hbm.1, s32[512]{0:T(512)} %slot_ref.1, ...), custom_call_target="tpu_custom_call" | custom-call | tf_op jit(solution)/shard_map/whole/pallas_call | solution.py:546
  99.8 1.7 %copy.12 = bf16[128,1024]{1,0:T(8,128)(2,1)} copy(bf16[128,1024]{1,0:T(8,128)(2,1)} %whole.1) | data formatting | bytes 524288
